TPU v7x, 32 devices: a whole 2x2x4 slice. The times are simulated.
32 devices in a mesh: blk: 4 (over z), wa: 8 (over y, x, core).
Axes of the slice: x: 2, y: 2, z: 4, core: 2. Of those that a mesh axis runs over, the one named last changes fastest.
Arguments:
- tokens: bfloat16 [8, 16, 64, 256], P('wa', 'blk'), may hold values from -6 to 6
- placement: int32 [8, 16], P('wa'), may hold values from 0 to 15, as said below
- block_mask: int32 [4, 8, 8], replicated, may hold values from 0 to 1, as said below
- w_qkv: bfloat16 [2, 256, 768], P(None, ('blk', 'wa')), may hold values from -0.375 to 0.375
- w_out: bfloat16 [2, 256, 256], P(None, ('blk', 'wa')), may hold values from -1.5 to 1.5
- w_in: bfloat16 [2, 256, 1024], P(None, ('blk', 'wa')), may hold values from -0.375 to 0.375
- w_down: bfloat16 [2, 1024, 256], P(None, ('blk', 'wa')), may hold values from -0.1875 to 0.1875
- biases: bfloat16 [2, 2560], P(None, ('blk', 'wa')), may hold values from -1.796875 to 1.796875
- gains: bfloat16 [2, 512], P(None, ('blk', 'wa')), may hold values from 0.5 to 1.5
- mask_logits: bfloat16 [2, 256], P(None, ('blk', 'wa')), may hold values from -3 to 1
- masked_pos: int32 [8, 4, 64], P('wa', 'blk'), may hold values from 0 to 255, as said below
- masked_count: int32 [8, 4], P('wa', 'blk'), may hold values from 17 to 64, as said below
- masked_grad: float32 [8, 4, 64, 256], P('wa', 'blk'), may hold values from -6 to 6
Outputs:
- out: float32 [8, 16, 64, 256], P('wa', 'blk')
- grad_tokens: float32 [8, 16, 64, 256], P('wa', 'blk')
- grad_w_qkv: float32 [2, 256, 768], P(None, ('blk', 'wa'))
- grad_w_out: float32 [2, 256, 256], P(None, ('blk', 'wa'))
- grad_w_in: float32 [2, 256, 1024], P(None, ('blk', 'wa'))
- grad_w_down: float32 [2, 1024, 256], P(None, ('blk', 'wa'))
- grad_biases: float32 [2, 2560], P(None, ('blk', 'wa'))
- grad_gains: float32 [2, 512], P(None, ('blk', 'wa'))
- grad_mask_logits: float32 [2, 256], P(None, ('blk', 'wa'))
Inputs may be any that keep to these rules, and one draw needn't show every extreme that they name: Each row of placement is a permutation of the 16 blocks of the group's 16 // 8 sequences. block_mask[h, i, i] = 1 for every head h and block i. `masked_pos`: the 64 entries of one device's list are distinct local rows. The first masked_count[g, b] entries of device (g, b)'s list are its masked rows; the other entries carry no gradient.
All inputs are finite; a program needn't handle non-finite values.
Results may differ from a plain program's by a relative error of at most 0.017.
Values may be sent and summed in bfloat16 or wider, within the bound.
A program may use at most 128 MiB of HBM per device.

v0:
```python
import jax
import jax.numpy as jnp
from jax import lax
from jax.sharding import PartitionSpec as P

HD = 64
NB = 8


HIGHEST = lax.Precision.HIGHEST


def normalize(hidden, norm_gain, norm_shift):
    row_mean = jnp.mean(hidden, axis=-1, keepdims=True)
    centred = hidden - row_mean
    row_var = jnp.mean(centred * centred, axis=-1, keepdims=True)
    return centred * lax.rsqrt(row_var + 1e-05) * norm_gain + norm_shift


def gelu_exact(values):
    return jax.nn.gelu(values, approximate=False)


def matmul(left, right):
    return jnp.dot(left, right, preferred_element_type=jnp.float32)


def contract_rows(left, right):
    return lax.dot_general(
        left, right, (((0,), (0,)), ((), ())), preferred_element_type=jnp.float32
    )


def times_transposed(left, right):
    return lax.dot_general(
        left, right, (((1,), (1,)), ((), ())), preferred_element_type=jnp.float32
    )


def unpack(weights, model_width):
    bias_all = weights[4].astype(jnp.float32)
    gain_all = weights[5].astype(jnp.float32)
    hidden_width = weights[2].shape[1]
    cuts = [
        0,
        model_width,
        2 * model_width,
        3 * model_width,
        4 * model_width,
        4 * model_width + hidden_width,
        5 * model_width + hidden_width,
        6 * model_width + hidden_width,
    ]
    pieces = [bias_all[cuts[index_cut] : cuts[index_cut + 1]] for index_cut in range(7)]
    return pieces + [gain_all[:model_width], gain_all[model_width:]]


def fetch_forward(layer_index, w_qkv, w_out, w_in, w_down, biases, gains, mask_logits):
    return (
        lax.all_gather(w_qkv[layer_index], ("blk", "wa"), axis=0, tiled=True),
        lax.all_gather(w_out[layer_index], ("blk", "wa"), axis=0, tiled=True),
        lax.all_gather(w_in[layer_index], ("blk", "wa"), axis=0, tiled=True),
        lax.all_gather(w_down[layer_index], ("blk", "wa"), axis=0, tiled=True),
        lax.all_gather(biases[layer_index], ("blk", "wa"), axis=0, tiled=True),
        lax.all_gather(gains[layer_index], ("blk", "wa"), axis=0, tiled=True),
        lax.all_gather(mask_logits[layer_index], ("blk", "wa"), axis=0, tiled=True),
    )


def fetch_again(layer_index, w_qkv, w_out, w_in, w_down, biases, gains, mask_logits):
    return (
        lax.all_gather(w_qkv[layer_index], ("blk", "wa"), axis=0, tiled=True),
        lax.all_gather(w_out[layer_index], ("blk", "wa"), axis=0, tiled=True),
        lax.all_gather(w_in[layer_index], ("blk", "wa"), axis=0, tiled=True),
        lax.all_gather(w_down[layer_index], ("blk", "wa"), axis=0, tiled=True),
        lax.all_gather(biases[layer_index], ("blk", "wa"), axis=0, tiled=True),
        lax.all_gather(gains[layer_index], ("blk", "wa"), axis=0, tiled=True),
        lax.all_gather(mask_logits[layer_index], ("blk", "wa"), axis=0, tiled=True),
    )


def tables(placement, block_mask):
    slot_order = placement[0]
    group_size = slot_order.shape[0]
    per_device = group_size // lax.axis_size("blk")
    inverse = (
        jnp.zeros((group_size,), jnp.int32)
        .at[slot_order]
        .set(jnp.arange(group_size, dtype=jnp.int32))
    )
    my_blocks = lax.dynamic_slice_in_dim(slot_order, lax.axis_index("blk") * per_device, per_device)
    sequence = my_blocks // NB
    position = my_blocks % NB
    block_ids = jnp.arange(NB, dtype=jnp.int32)
    key_slots = inverse[sequence[:, None] * NB + block_ids[None, :]]
    onehot = (position[:, None] == block_ids[None, :]).astype(jnp.float32)
    allowed = (
        jnp.einsum("bq,hqk->bhk", onehot, block_mask.astype(jnp.float32), precision=HIGHEST) > 0.5
    )
    return (key_slots, onehot, allowed)


def score_terms(logits, onehot, allowed, block_rows):
    logit_table = logits.astype(jnp.float32).reshape(allowed.shape[1], NB, NB)
    row_bias = jnp.einsum("bq,hqk->bhk", onehot, jax.nn.log_sigmoid(logit_table), precision=HIGHEST)
    score_bias = jnp.repeat(row_bias, block_rows, axis=2)[:, :, None, :]
    keep_mask = jnp.repeat(allowed, block_rows, axis=2)[:, :, None, :]
    return (logit_table, score_bias, keep_mask)


def split_heads(qkv, seq_pairs, model_width, block_rows):
    blocks = seq_pairs.shape[0]
    head_count = model_width // HD
    queries = qkv[:, :model_width].reshape(blocks, block_rows, head_count, HD)
    key_rows = seq_pairs[:, :, :model_width].reshape(blocks, seq_pairs.shape[1], head_count, HD)
    values = seq_pairs[:, :, model_width:].reshape(blocks, seq_pairs.shape[1], head_count, HD)
    return (queries, key_rows, values)


def scores_of(queries, key_rows, score_bias, keep_mask):
    raw = (
        jnp.einsum("bqhd,bkhd->bhqk", queries, key_rows, preferred_element_type=jnp.float32) * 0.125
    )
    return jnp.where(keep_mask, raw + score_bias, -1e30)


def layer_forward(row_data, weights, key_slots, onehot, allowed, block_rows):
    w_qkv, w_out, w_in, w_down, biases, gains, logits = weights
    model_width = row_data.shape[1]
    b_query, b_value, b_output, shift_one, b_inner, b_down, shift_two, gain_one, gain_two = unpack(
        weights, model_width
    )
    blocks = key_slots.shape[0]
    low_rows = row_data.astype(jnp.bfloat16)
    bias_qkv = jnp.concatenate([b_query, jnp.zeros((model_width,), jnp.float32), b_value])
    qkv = (matmul(low_rows, w_qkv) + bias_qkv).astype(jnp.bfloat16)
    key_pairs = qkv[:, model_width:].reshape(blocks, block_rows, 2 * model_width)
    group_pairs = lax.all_gather(key_pairs, "blk", axis=0, tiled=True)
    seq_pairs = group_pairs[key_slots].reshape(blocks, NB * block_rows, 2 * model_width)
    queries, key_rows, values = split_heads(qkv, seq_pairs, model_width, block_rows)
    logit_table, score_bias, keep_mask = score_terms(logits, onehot, allowed, block_rows)
    scores = scores_of(queries, key_rows, score_bias, keep_mask)
    row_max = jnp.max(scores, axis=-1, keepdims=True)
    log_total = row_max + jnp.log(jnp.sum(jnp.exp(scores - row_max), axis=-1, keepdims=True))
    attn_probs = jnp.exp(scores - log_total).astype(jnp.bfloat16)
    attended = jnp.einsum("bhqk,bkhd->bqhd", attn_probs, values, preferred_element_type=jnp.float32)
    attended = attended.astype(jnp.bfloat16).reshape(-1, model_width)
    first_sum = row_data + matmul(attended, w_out) + b_output
    normed = normalize(first_sum, gain_one, shift_one)
    feed_inner = matmul(normed.astype(jnp.bfloat16), w_in) + b_inner
    feed_act = gelu_exact(feed_inner).astype(jnp.bfloat16)
    second = normed + matmul(feed_act, w_down) + b_down
    result = normalize(second, gain_two, shift_two)
    saved = (low_rows, qkv, seq_pairs, log_total, attended, first_sum, feed_inner, second)
    return (result, saved)


def rows_backward(d_result, first_sum, feed_inner, second, attended, weights):
    w_qkv, w_out, w_in, w_down, biases, gains, logits = weights
    model_width = first_sum.shape[1]
    b_query, b_value, b_output, shift_one, b_inner, b_down, shift_two, gain_one, gain_two = unpack(
        weights, model_width
    )
    pull_second = jax.vjp(normalize, second, gain_two, shift_two)[1]
    d_second, d_gain_two, d_shift_two = pull_second(d_result)
    d_feed = d_second.astype(jnp.bfloat16)
    normed, pull_first = jax.vjp(normalize, first_sum, gain_one, shift_one)
    feed_act, pull_act = jax.vjp(gelu_exact, feed_inner)
    grad_down = contract_rows(feed_act.astype(jnp.bfloat16), d_feed)
    d_act = times_transposed(d_feed, w_down)
    d_inner = pull_act(d_act)[0].astype(jnp.bfloat16)
    grad_in = contract_rows(normed.astype(jnp.bfloat16), d_inner)
    d_normed = times_transposed(d_inner, w_in) + d_second
    d_first, d_gain_one, d_shift_one = pull_first(d_normed)
    d_branch = d_first.astype(jnp.bfloat16)
    grad_out = contract_rows(attended, d_branch)
    d_attended = times_transposed(d_branch, w_out).astype(jnp.bfloat16)
    grad_sums = (
        grad_out,
        grad_in,
        grad_down,
        jnp.sum(d_branch.astype(jnp.float32), axis=0),
        jnp.sum(d_inner.astype(jnp.float32), axis=0),
        jnp.sum(d_feed.astype(jnp.float32), axis=0),
        d_gain_one,
        d_shift_one,
        d_gain_two,
        d_shift_two,
    )
    return (d_attended, d_first, grad_sums)


def attention_backward(
    d_attended,
    qkv,
    seq_pairs,
    log_total,
    logits,
    key_slots,
    onehot,
    allowed,
    block_rows,
    group_size,
):
    model_width = d_attended.shape[1]
    blocks = key_slots.shape[0]
    head_count = model_width // HD
    queries, key_rows, values = split_heads(qkv, seq_pairs, model_width, block_rows)
    logit_table, score_bias, keep_mask = score_terms(logits, onehot, allowed, block_rows)
    scores = scores_of(queries, key_rows, score_bias, keep_mask)
    attn_probs = jnp.exp(scores - log_total)
    d_heads = d_attended.reshape(blocks, block_rows, head_count, HD)
    d_probs = jnp.einsum("bqhd,bkhd->bhqk", d_heads, values, preferred_element_type=jnp.float32)
    inner_sum = jnp.sum(attn_probs * d_probs, axis=-1, keepdims=True)
    d_scores = (attn_probs * (d_probs - inner_sum)).astype(jnp.bfloat16)
    per_block = (
        d_scores.astype(jnp.float32)
        .reshape(blocks, head_count, block_rows, NB, block_rows)
        .sum(axis=(2, 4))
    )
    d_logits = jnp.einsum("bq,bhk->hqk", onehot, per_block, precision=HIGHEST) * jax.nn.sigmoid(
        -logit_table
    )
    d_query = (
        jnp.einsum("bhqk,bkhd->bqhd", d_scores, key_rows, preferred_element_type=jnp.float32)
        * 0.125
    )
    d_keys = (
        jnp.einsum("bhqk,bqhd->bkhd", d_scores, queries, preferred_element_type=jnp.float32) * 0.125
    )
    d_values = jnp.einsum(
        "bhqk,bqhd->bkhd",
        attn_probs.astype(jnp.bfloat16),
        d_heads,
        preferred_element_type=jnp.float32,
    )
    seq_len = seq_pairs.shape[1]
    d_pairs = jnp.concatenate(
        [
            d_keys.reshape(blocks, seq_len, model_width),
            d_values.reshape(blocks, seq_len, model_width),
        ],
        axis=-1,
    )
    d_pairs = d_pairs.reshape(blocks * NB, block_rows, 2 * model_width)
    grad_table = (
        jnp.zeros((group_size, block_rows, 2 * model_width), jnp.float32)
        .at[key_slots.reshape(-1)]
        .add(d_pairs)
    )
    d_owned = lax.psum_scatter(
        grad_table.astype(jnp.bfloat16), "blk", scatter_dimension=0, tiled=True
    ).astype(jnp.float32)
    return (
        d_query.reshape(-1, model_width),
        d_owned.reshape(-1, 2 * model_width),
        d_logits.reshape(-1),
    )


def local(
    tokens,
    placement,
    block_mask,
    w_qkv,
    w_out,
    w_in,
    w_down,
    biases,
    gains,
    mask_logits,
    masked_pos,
    masked_count,
    masked_grad,
):
    layer_total = w_qkv.shape[0]
    model_width = tokens.shape[-1]
    block_rows = tokens.shape[2]
    group_size = placement.shape[1]
    key_slots, onehot, allowed = tables(placement, block_mask)
    row_data = tokens.reshape(-1, model_width).astype(jnp.float32)
    kept_weights = []
    saved_all = []
    for layer_index in range(layer_total):
        weights = fetch_forward(layer_index, w_qkv, w_out, w_in, w_down, biases, gains, mask_logits)
        kept_weights.append(weights)
        row_data, saved = layer_forward(row_data, weights, key_slots, onehot, allowed, block_rows)
        saved_all.append(saved)
    result = row_data.reshape(tokens.shape)
    chosen = masked_pos[0, 0]
    live_rows = (jnp.arange(chosen.shape[0]) < masked_count[0, 0]).astype(jnp.float32)
    listed = masked_grad[0, 0] * live_rows[:, None]
    d_rows = None
    layer_grads = [None] * layer_total
    for layer_index in reversed(range(layer_total)):
        weights = fetch_again(layer_index, w_qkv, w_out, w_in, w_down, biases, gains, mask_logits)
        low_rows, qkv, seq_pairs, log_total, attended, first_sum, feed_inner, second = saved_all[
            layer_index
        ]
        if layer_index == layer_total - 1:
            dense_grad = jnp.zeros(first_sum.shape, jnp.float32).at[chosen].set(listed)
            d_attended, d_first, grad_sums = rows_backward(
                dense_grad, first_sum, feed_inner, second, attended, weights
            )
        else:
            d_attended, d_first, grad_sums = rows_backward(
                d_rows, first_sum, feed_inner, second, attended, weights
            )
        d_query, d_owned, d_logits = attention_backward(
            d_attended,
            qkv,
            seq_pairs,
            log_total,
            weights[6],
            key_slots,
            onehot,
            allowed,
            block_rows,
            group_size,
        )
        d_qkv = jnp.concatenate([d_query, d_owned], axis=1).astype(jnp.bfloat16)
        grad_qkv = contract_rows(low_rows, d_qkv)
        d_rows = times_transposed(d_qkv, weights[0]) + d_first
        column_sums = jnp.sum(d_qkv.astype(jnp.float32), axis=0)
        (
            grad_out,
            grad_in,
            grad_down,
            d_b_output,
            d_b_inner,
            d_b_down,
            d_gain_one,
            d_shift_one,
            d_gain_two,
            d_shift_two,
        ) = grad_sums
        bias_grad = jnp.concatenate(
            [
                column_sums[:model_width],
                column_sums[2 * model_width :],
                d_b_output,
                d_shift_one,
                d_b_inner,
                d_b_down,
                d_shift_two,
            ]
        )
        gain_grad = jnp.concatenate([d_gain_one, d_gain_two])
        layer_grads[layer_index] = (
            lax.psum_scatter(grad_qkv, ("blk", "wa"), scatter_dimension=0, tiled=True),
            lax.psum_scatter(grad_out, ("blk", "wa"), scatter_dimension=0, tiled=True),
            lax.psum_scatter(grad_in, ("blk", "wa"), scatter_dimension=0, tiled=True),
            lax.psum_scatter(grad_down, ("blk", "wa"), scatter_dimension=0, tiled=True),
            lax.psum_scatter(bias_grad, ("blk", "wa"), scatter_dimension=0, tiled=True),
            lax.psum_scatter(gain_grad, ("blk", "wa"), scatter_dimension=0, tiled=True),
            lax.psum_scatter(d_logits, ("blk", "wa"), scatter_dimension=0, tiled=True),
        )
    stacked = [
        jnp.stack([layer_grads[layer_index][member] for layer_index in range(layer_total)])
        for member in range(7)
    ]
    grad_tokens = d_rows.reshape(tokens.shape)
    return (
        result,
        grad_tokens,
        stacked[0],
        stacked[1],
        stacked[2],
        stacked[3],
        stacked[4],
        stacked[5],
        stacked[6],
    )


def solution(mesh):
    placed = (
        P("wa", "blk", None, None),
        P("wa", None),
        P(),
        P(None, ("blk", "wa"), None),
        P(None, ("blk", "wa"), None),
        P(None, ("blk", "wa"), None),
        P(None, ("blk", "wa"), None),
        P(None, ("blk", "wa")),
        P(None, ("blk", "wa")),
        P(None, ("blk", "wa")),
        P("wa", "blk", None),
        P("wa", "blk"),
        P("wa", "blk", None, None),
    )
    return jax.shard_map(
        local,
        mesh=mesh,
        in_specs=placed,
        out_specs=(
            P("wa", "blk", None, None),
            P("wa", "blk", None, None),
            P(None, ("blk", "wa"), None),
            P(None, ("blk", "wa"), None),
            P(None, ("blk", "wa"), None),
            P(None, ("blk", "wa"), None),
            P(None, ("blk", "wa")),
            P(None, ("blk", "wa")),
            P(None, ("blk", "wa")),
        ),
        check_vma=False,
    )
```

profile of v0, /device:TPU:1, one launch (start us, length us, event | category | flops | bytes accessed | tf_op | source)
XLA Modules:
  0.0 1563.3 jit_solution(13530253955506145877)
XLA Ops:
  10.8 41.3 %all-reduce.13 = (bf16[2560]{0:T(1024)(128)(2,1)S(1)}, bf16[2560]{0:T(1024)(128)(2,1)S(1)}, bf16[256]{0:T(256)(128)(2,1)S(1)}, bf16[512]{0:T(512)(128)(2,1)S(1)}...) all-reduce(bf16[2560]{0:T(1024)(128)(2,1)S(1)} %dynamic-update-slice,, ...), channel_id=3, replica_groups=mesh['blk'=4,'wa'=8] {'blk','wa'}, use_global_device_ids=true, to_apply=%add | all-reduce | flops 6656 | bytes 26624
  54.1 42.7 %all-gather = bf16[1,256,768]{2,1,0:T(8,128)(2,1)S(1)} all-gather(bf16[1,8,768]{2,1,0:T(8,128)(2,1)S(1)} %get-tuple-element.95), channel_id=2, replica_groups=mesh['blk'=4,'wa'=8] {'blk','wa'}, dimensions={1}, use_global_device_ids=true | all-gather | bytes 405504 | tf_op jit(solution)/shard_map/all_gather | solution.py:60
  105.8 40.1 %all-gather.3 = bf16[1,256,256]{2,1,0:T(8,128)(2,1)} all-gather(bf16[1,8,256]{2,1,0:T(8,128)(2,1)S(1)} %get-tuple-element.110), channel_id=5, replica_groups=mesh['blk'=4,'wa'=8] {'blk','wa'}, dimensions={1}, use_global_device_ids=true | all-gather | bytes 135168 | tf_op jit(solution)/shard_map/all_gather | solution.py:61
  145.9 41.8 %all-gather.7 = bf16[1,256,768]{2,1,0:T(8,128)(2,1)} all-gather(bf16[1,8,768]{2,1,0:T(8,128)(2,1)S(1)} %get-tuple-element.96), channel_id=9, replica_groups=mesh['blk'=4,'wa'=8] {'blk','wa'}, dimensions={1}, use_global_device_ids=true | all-gather | bytes 405504 | tf_op jit(solution)/shard_map/all_gather | solution.py:60
  189.4 40.7 %all-gather.5 = bf16[1,256,1024]{2,1,0:T(8,128)(2,1)} all-gather(bf16[1,8,1024]{2,1,0:T(8,128)(2,1)S(1)} %get-tuple-element.93), channel_id=7, replica_groups=mesh['blk'=4,'wa'=8] {'blk','wa'}, dimensions={1}, use_global_device_ids=true | all-gather | bytes 540672 | tf_op jit(solution)/shard_map/all_gather | solution.py:62
  230.1 42.1 %all-gather.6 = bf16[1,1024,256]{2,1,0:T(8,128)(2,1)} all-gather(bf16[1,32,256]{2,1,0:T(8,128)(2,1)S(1)} %get-tuple-element.92), channel_id=8, replica_groups=mesh['blk'=4,'wa'=8] {'blk','wa'}, dimensions={1}, use_global_device_ids=true | all-gather | bytes 540672 | tf_op jit(solution)/shard_map/all_gather | solution.py:63
  282.1 4.4 multiply_convert_fusion.3
  292.2 40.0 %all-gather.10 = bf16[1,256,256]{2,1,0:T(8,128)(2,1)} all-gather(bf16[1,8,256]{2,1,0:T(8,128)(2,1)S(1)} %copy-done.87), channel_id=12, replica_groups=mesh['blk'=4,'wa'=8] {'blk','wa'}, dimensions={1}, use_global_device_ids=true | all-gather | bytes 135168 | tf_op jit(solution)/shard_map/all_gather | solution.py:61
  333.4 51.4 %all-gather.12 = bf16[1,256,1024]{2,1,0:T(8,128)(2,1)} all-gather(bf16[1,8,1024]{2,1,0:T(8,128)(2,1)S(1)} %copy-done.59), channel_id=14, replica_groups=mesh['blk'=4,'wa'=8] {'blk','wa'}, dimensions={1}, use_global_device_ids=true | all-gather | bytes 540672 | tf_op jit(solution)/shard_map/all_gather | solution.py:62
  384.9 40.8 %all-gather.13 = bf16[1,1024,256]{2,1,0:T(8,128)(2,1)} all-gather(bf16[1,32,256]{2,1,0:T(8,128)(2,1)S(1)} %copy-done.60), channel_id=15, replica_groups=mesh['blk'=4,'wa'=8] {'blk','wa'}, dimensions={1}, use_global_device_ids=true | all-gather | bytes 540672 | tf_op jit(solution)/shard_map/all_gather | solution.py:63
  441.7 3.6 multiply_convert_fusion.2
  466.2 5.2 concatenate.44
  471.4 4.3 copy.147
  475.7 4.7 concatenate.45
  480.4 7.8 pad_maximum_fusion
  488.2 6.9 copy.148
  496.7 9.7 scatter_fusion
  516.7 16.3 %reduce-scatter.15.cloned.1.call-done = bf16[4,64,512]{2,1,0:T(8,128)(2,1)} async-done(((bf16[16,64,512]{2,1,0:T(8,128)(2,1)}), bf16[4,64,512]{2,1,0:T(8,128)(2,1)}) %reduce-scatter.15.cloned.1.call-update) | async-done | bytes 262160 | tf_op jit(solution)/shard_map/reduce_scatter | solution.py:251
  560.2 5.0 concatenate.48
  570.7 7.8 pad_maximum_fusion.1
  578.5 6.9 copy.155
  586.0 6.5 scatter_fusion.1
  614.3 48.1 %reduce-scatter.21.cloned.1.call-done = f32[8,256]{1,0:T(8,128)} async-done(((f32[256,256]{1,0:T(8,128)}), f32[8,256]{1,0:T(8,128)}) %reduce-scatter.21.cloned.1.call-update) | async-done | bytes 8208 | tf_op jit(solution)/shard_map/reduce_scatter | solution.py:351
  662.4 131.4 %reduce-scatter.19.cloned.1.call-done = f32[8,256]{1,0:T(8,128)} async-done(((f32[256,256]{1,0:T(8,128)}), f32[8,256]{1,0:T(8,128)}) %reduce-scatter.19.cloned.1.call-update) | async-done | bytes 8208 | tf_op jit(solution)/shard_map/reduce_scatter | solution.py:351
  795.1 99.5 %reduce-scatter.33.cloned.1.call-done = f32[8,768]{1,0:T(8,128)} async-done(((f32[256,768]{1,0:T(8,128)}), f32[8,768]{1,0:T(8,128)}) %reduce-scatter.33.cloned.1.call-update) | async-done | bytes 24592
  895.7 29.1 %reduce-scatter.17.cloned.1.call-done = bf16[4,64,512]{2,1,0:T(8,128)(2,1)} async-done(((bf16[16,64,512]{2,1,0:T(8,128)(2,1)}), bf16[4,64,512]{2,1,0:T(8,128)(2,1)}) %reduce-scatter.17.cloned.1.call-update) | async-done | bytes 262160 | tf_op jit(solution)/shard_map/reduce_scatter | solution.py:251
  927.5 38.9 %all-reduce.12 = (f32[2560]{0:T(1024)S(1)}, f32[2560]{0:T(1024)S(1)}, f32[512]{0:T(512)S(1)}, f32[512]{0:T(512)S(1)}, f32[256]{0:T(256)S(1)}, /*index=5*/f32[256]{0:T(256)S(1)}) all-reduce(f32[2560]{0:T(1024)S(1)} %constant_dynamic-update-slice_fusion.1, ...), channel_id=27, replica_groups=mesh['blk'=4,'wa'=8] {'blk','wa'}, use_global_device_ids=true, to_apply=%region_49.50.clone | all-reduce | flops 6656 | bytes 53248
  968.6 86.9 %reduce-scatter.29.cloned.1.call-done = f32[32,256]{1,0:T(8,128)} async-done(((f32[1024,256]{1,0:T(8,128)}), f32[32,256]{1,0:T(8,128)}) %reduce-scatter.29.cloned.1.call-update) | async-done | bytes 32784 | tf_op jit(solution)/shard_map/reduce_scatter | solution.py:353
  1055.5 133.1 %reduce-scatter.27.cloned.1.call-done = f32[32,256]{1,0:T(8,128)} async-done(((f32[1024,256]{1,0:T(8,128)}), f32[32,256]{1,0:T(8,128)}) %reduce-scatter.27.cloned.1.call-update) | async-done | bytes 32784 | tf_op jit(solution)/shard_map/reduce_scatter | solution.py:353
  1190.0 131.4 %reduce-scatter.25.cloned.1.call-done = f32[8,1024]{1,0:T(8,128)} async-done(((f32[256,1024]{1,0:T(8,128)}), f32[8,1024]{1,0:T(8,128)}) %reduce-scatter.25.cloned.1.call-update) | async-done | bytes 32784 | tf_op jit(solution)/shard_map/reduce_scatter | solution.py:352
  1321.4 133.1 %reduce-scatter.23.cloned.1.call-done = f32[8,1024]{1,0:T(8,128)} async-done(((f32[256,1024]{1,0:T(8,128)}), f32[8,1024]{1,0:T(8,128)}) %reduce-scatter.23.cloned.1.call-update) | async-done | bytes 32784 | tf_op jit(solution)/shard_map/reduce_scatter | solution.py:352
  1457.0 97.6 %reduce-scatter.31.cloned.1.call-done = f32[8,768]{1,0:T(8,128)} async-done(((f32[256,768]{1,0:T(8,128)}), f32[8,768]{1,0:T(8,128)}) %reduce-scatter.31.cloned.1.call-update) | async-done | bytes 24592
  (510 shorter events, 147.4 us)
Async XLA Ops:
  7.2 92.4 %copy-start.122 = (s32[1,16]{1,0:T(1,128)S(1)}, s32[1,16]{1,0:T(1,128)}, u32[]{:S(2)}) copy-start(s32[1,16]{1,0:T(1,128)} %param.14) | copy-start | bytes 196
  7.2 265.0 %all-gather.17.cloned.1.call-start = ((), (), s32[]{:S(2)}) async-start(), calls=%async_computation.10 | async-start | bytes 1310720 | tf_op jit(solution)/shard_map/all_gather | solution.py:138
  54.1 48.2 %copy-start.128 = (s32[4,8,8]{2,1,0:T(8,128)S(1)}, s32[4,8,8]{2,1,0:T(8,128)}, u32[]{:S(2)}) copy-start(s32[4,8,8]{2,1,0:T(8,128)} %param.15) | copy-start | bytes 3076
  99.5 326.6 %all-gather.19.cloned.1.call-start = ((), (), s32[]{:S(2)}) async-start(), calls=%async_computation.11 | async-start | bytes 1310720 | tf_op jit(solution)/shard_map/all_gather | solution.py:138
  100.5 87.7 %copy-start.67 = (bf16[2,8,1024]{2,1,0:T(8,128)(2,1)S(1)}, bf16[2,8,1024]{2,1,0:T(8,128)(2,1)}, u32[]{:S(2)}) copy-start(bf16[2,8,1024]{2,1,0:T(8,128)(2,1)} %param.18) | copy-start | bytes 98308
  100.6 88.3 %copy-start.68 = (bf16[2,32,256]{2,1,0:T(8,128)(2,1)S(1)}, bf16[2,32,256]{2,1,0:T(8,128)(2,1)}, u32[]{:S(2)}) copy-start(bf16[2,32,256]{2,1,0:T(8,128)(2,1)} %param.19) | copy-start | bytes 98308
  104.7 173.8 %copy-start.22 = (bf16[4,64,4,64]{1,3,2,0:T(8,128)(2,1)}, bf16[4,64,4,64]{1,3,2,0:T(8,128)(2,1)S(1)}, u32[]{:S(2)}) copy-start(bf16[4,64,4,64]{1,3,2,0:T(8,128)(2,1)S(1)} %copy.151) | copy-start | bytes 393220
  145.9 128.2 %copy-start.83 = (s32[1024]{0:T(1024)}, s32[1024]{0:T(1024)S(1)}, u32[]{:S(2)}) copy-start(s32[1024]{0:T(1024)S(1)} %pad_clamp_fusion) | copy-start | bytes 12292
  286.7 46.7 %copy-start.59 = (bf16[1,8,1024]{2,1,0:T(8,128)(2,1)S(1)}, bf16[1,8,1024]{2,1,0:T(8,128)(2,1)}, u32[]{:S(2)}) copy-start(bf16[1,8,1024]{2,1,0:T(8,128)(2,1)} %get-tuple-element.94) | copy-start | bytes 49156
  287.1 97.8 %copy-start.60 = (bf16[1,32,256]{2,1,0:T(8,128)(2,1)S(1)}, bf16[1,32,256]{2,1,0:T(8,128)(2,1)}, u32[]{:S(2)}) copy-start(bf16[1,32,256]{2,1,0:T(8,128)(2,1)} %get-tuple-element.91) | copy-start | bytes 49156
  288.1 138.0 %copy-start.84 = (s32[1024]{0:T(1024)S(1)}, s32[1024]{0:T(1024)}, u32[]{:S(2)}) copy-start(s32[1024]{0:T(1024)} %copy-done.83) | copy-start | bytes 12292
  288.9 244.2 %reduce-scatter.15.cloned.1.call-start = ((), (), s32[]{:S(2)}) async-start(), calls=%async_computation.12 | async-start | bytes 1310720 | tf_op jit(solution)/shard_map/reduce_scatter | solution.py:251
  509.1 153.2 %reduce-scatter.21.cloned.1.call-start = ((), (), s32[]{:S(2)}) async-start(), calls=%async_computation.15 | async-start | bytes 270336 | tf_op jit(solution)/shard_map/reduce_scatter | solution.py:351
  516.7 277.1 %reduce-scatter.19.cloned.1.call-start = ((), (), s32[]{:S(2)}) async-start(), calls=%async_computation.14 | async-start | bytes 270336 | tf_op jit(solution)/shard_map/reduce_scatter | solution.py:351
  548.1 346.5 %reduce-scatter.33.cloned.1.call-start = ((), (), s32[]{:S(2)}) async-start(), calls=%async_computation.21 | async-start | bytes 811008
  554.1 370.6 %reduce-scatter.17.cloned.1.call-start = ((), (), s32[]{:S(2)}) async-start(), calls=%async_computation.13 | async-start | bytes 1310720 | tf_op jit(solution)/shard_map/reduce_scatter | solution.py:251
  593.7 461.8 %reduce-scatter.29.cloned.1.call-start = ((), (), s32[]{:S(2)}) async-start(), calls=%async_computation.19 | async-start | bytes 1081344 | tf_op jit(solution)/shard_map/reduce_scatter | solution.py:353
  596.2 592.4 %reduce-scatter.27.cloned.1.call-start = ((), (), s32[]{:S(2)}) async-start(), calls=%async_computation.18 | async-start | bytes 1081344 | tf_op jit(solution)/shard_map/reduce_scatter | solution.py:353
  597.7 723.8 %reduce-scatter.25.cloned.1.call-start = ((), (), s32[]{:S(2)}) async-start(), calls=%async_computation.17 | async-start | bytes 1081344 | tf_op jit(solution)/shard_map/reduce_scatter | solution.py:352
  599.3 855.3 %reduce-scatter.23.cloned.1.call-start = ((), (), s32[]{:S(2)}) async-start(), calls=%async_computation.16 | async-start | bytes 1081344 | tf_op jit(solution)/shard_map/reduce_scatter | solution.py:352
  613.4 941.2 %reduce-scatter.31.cloned.1.call-start = ((), (), s32[]{:S(2)}) async-start(), calls=%async_computation.20 | async-start | bytes 811008
  614.1 313.3 %copy-start.91 = (f32[2560]{0:T(1024)S(1)}, f32[2560]{0:T(1024)}, u32[]{:S(2)}) copy-start(f32[2560]{0:T(1024)} %custom-call.1) | copy-start | bytes 30724
  614.1 313.3 %copy-start.111 = (f32[256]{0:T(256)S(1)}, f32[256]{0:T(256)}, u32[]{:S(2)}) copy-start(f32[256]{0:T(256)} %get-tuple-element.66) | copy-start | bytes 3076
  614.1 313.3 %copy-start.110 = (f32[256]{0:T(256)S(1)}, f32[256]{0:T(256)}, u32[]{:S(2)}) copy-start(f32[256]{0:T(256)} %get-tuple-element.44) | copy-start | bytes 3076
  614.2 313.3 %copy-start.118 = (f32[1024]{0:T(1024)S(1)}, f32[1024]{0:T(1024)}, u32[]{:S(2)}) copy-start(f32[1024]{0:T(1024)} %get-tuple-element.150) | copy-start | bytes 12292
  614.2 313.3 %copy-start.109 = (f32[256]{0:T(256)S(1)}, f32[256]{0:T(256)}, u32[]{:S(2)}) copy-start(f32[256]{0:T(256)} %get-tuple-element.64) | copy-start | bytes 3076
  614.2 313.3 %copy-start.124 = (f32[256]{0:T(256)S(1)}, f32[256]{0:T(256)}, u32[]{:S(2)}) copy-start(f32[256]{0:T(256)} %get-tuple-element.45) | copy-start | bytes 3076
  614.3 313.2 %copy-start.104 = (f32[512]{0:T(512)S(1)}, f32[512]{0:T(512)}, u32[]{:S(2)}) copy-start(f32[512]{0:T(512)} %pad_maximum_fusion.15) | copy-start | bytes 6148
  614.3 313.2 %copy-start.116 = (f32[256]{0:T(256)S(1)}, f32[256]{0:T(256)}, u32[]{:S(2)}) copy-start(f32[256]{0:T(256)} %reshape.510) | copy-start | bytes 3076
  924.8 531.2 %copy-start.17 = (bf16[1,256,768]{2,1,0:T(8,128)(2,1)S(1)}, bf16[1,256,768]{2,1,0:T(8,128)(2,1)}, u32[]{:S(2)}) copy-start(bf16[1,256,768]{2,1,0:T(8,128)(2,1)} %copy-done.16) | copy-start | bytes 1179652
  924.8 531.2 %copy-start.20 = (f32[256,256]{1,0:T(8,128)S(1)}, f32[256,256]{1,0:T(8,128)}, u32[]{:S(2)}) copy-start(f32[256,256]{1,0:T(8,128)} %copy-done.19) | copy-start | bytes 786436
  924.8 531.2 %copy-start.101 = (f32[256]{0:T(256)S(1)}, f32[256]{0:T(256)}, u32[]{:S(2)}) copy-start(f32[256]{0:T(256)} %copy-done.100) | copy-start | bytes 3076
  (112 other events, 541.6 us)
Sparse Core Ops, SparseCore 0:
  99.6 23.7 all-gather.16
  289.0 23.7 all-gather.18
  509.2 23.8 reduce-scatter.14
  535.2 127.0 reduce-scatter.20
  664.4 129.3 reduce-scatter.18
  799.6 95.0 reduce-scatter.32
  897.0 27.6 reduce-scatter.16
  927.0 128.4 reduce-scatter.28
  1057.8 130.7 reduce-scatter.26
  1190.7 130.7 reduce-scatter.24
  1323.8 130.7 reduce-scatter.22
  1459.5 95.0 reduce-scatter.30
where the time goes:
time: 1570 us; the launch traced here: 1560 us
  waiting for transfers between devices  907 us (58%)
  blocking collectives  420 us (27%)
  local copies, waits for them, and re-layouts  103 us (7%)
  other arithmetic  60.3 us (4%)
  matrix products  55.7 us (4%)
  between operations  16.9 us (1%)
    reduce_scatter x2, waiting for transfers between devices, local(): lax.psum_scatter(grad_in, ('blk', 'wa'), scatter_dimension=0, tiled=True)  265 us
    reduce_scatter x2, waiting for transfers between devices, local(): lax.psum_scatter(grad_down, ('blk', 'wa'), scatter_dimension=0, tiled=True)  220 us
    unnamed x14, waiting for transfers between devices  197 us
    reduce_scatter x2, waiting for transfers between devices, local(): lax.psum_scatter(grad_out, ('blk', 'wa'), scatter_dimension=0, tiled=True)  180 us
    all_gather x2, blocking collectives, fetch_forward(): lax.all_gather(w_in[layer_index], ('blk', 'wa'), axis=0, tiled=True)  92.1 us
    all_gather x2, blocking collectives, fetch_forward(): lax.all_gather(w_qkv[layer_index], ('blk', 'wa'), axis=0, tiled=True)  84.5 us
    all_gather x2, blocking collectives, fetch_forward(): lax.all_gather(w_down[layer_index], ('blk', 'wa'), axis=0, tiled=True)  82.9 us
    unnamed x2, blocking collectives  80.2 us
  transfers between devices with their start and end apart: 12, of which 10 were waited for; matrix products, arithmetic and copies ran while one was open for 7% of the time, Pallas kernels for 0%

commit v1 on v0

v1 whole, which is shorter than its diff:
```python
import functools

import jax
import jax.numpy as jnp
from jax import lax
from jax.experimental import pallas as pl
from jax.experimental.pallas import tpu as pltpu
from jax.sharding import PartitionSpec as P

D = 256
H = 4
HD = 64
FF = 1024
NB = 8
BS = 64
SEQ = 512
LAYERS = 2
BLK_DEV = 4
HALF = 256
MY_FF = FF // 2
NEG = -1e30
EPS = 1e-05
MESH = pl.DeviceIdType.MESH
F32 = jnp.float32
BF16 = jnp.bfloat16
HIGHEST = lax.Precision.HIGHEST

ROW_BQ, ROW_BV, ROW_BO, ROW_S1, ROW_BI, ROW_BD, ROW_S2, ROW_G1, ROW_G2 = 0, 2, 4, 6, 8, 16, 18, 20, 22
PV_ROWS = 24
SG_BQ, SG_BV, SG_BI, SG_BO, SG_S1, SG_BD, SG_S2, SG_G1, SG_G2, SG_LG = 0, 1, 2, 6, 8, 10, 12, 14, 16, 24
SG_ROWS = 40


def nn(left, right):
    return jnp.dot(left, right, preferred_element_type=F32)


def nt(left, right):
    return lax.dot_general(left, right, (((1,), (1,)), ((), ())), preferred_element_type=F32)


def tn(left, right):
    return lax.dot_general(left, right, (((0,), (0,)), ((), ())), preferred_element_type=F32)


def lanes(shape):
    return lax.broadcasted_iota(jnp.int32, shape, len(shape) - 1)


def turn(value, shift):
    return pltpu.roll(value, shift % 128, 1)


def pick_groups(first, second, core):
    if isinstance(core, int):
        if core == 1:
            first, second = turn(first, -32), turn(second, -32)
    else:
        first = jnp.where(core == 1, turn(first, -32), first)
        second = jnp.where(core == 1, turn(second, -32), second)
    group = lanes(first.shape) // 32
    return jnp.where(
        group == 0,
        first,
        jnp.where(group == 1, turn(first, -32), jnp.where(group == 2, turn(second, 64), turn(second, 32))),
    )


def weave_groups(zero, one):
    group = lanes(zero.shape) // 32
    first = jnp.where(
        group == 0, zero, jnp.where(group == 1, turn(one, 32), jnp.where(group == 2, turn(zero, 32), turn(one, 64)))
    )
    second = jnp.where(
        group == 0,
        turn(zero, -64),
        jnp.where(group == 1, turn(one, -32), jnp.where(group == 2, turn(zero, -32), one)),
    )
    return first, second


class Links:
    def __init__(self, send, recv, anyone):
        self.send, self.recv, self.anyone = send, recv, anyone
        self.send_used = self.recv_used = 0
        self.pending = {}

    def recv_sem(self):
        self.recv_used += 1
        return self.recv_used - 1

    def send_sem(self, bytes_like):
        self.send_used += 1
        self.pending[self.send_used - 1] = bytes_like
        return self.send_used - 1

    def push(self, source, target, send_sem, recv_sem, device):
        remote(source, target, self.send.at[send_sem], self.recv.at[recv_sem], device).start()

    def arrived(self, bytes_like, recv_sem):
        remote(bytes_like, bytes_like, self.send.at[0], self.recv.at[recv_sem], self.anyone).wait_recv()

    def drain(self):
        for send_sem, bytes_like in self.pending.items():
            remote(bytes_like, bytes_like, self.send.at[send_sem], self.recv.at[0], self.anyone).wait_send()


def remote(source, target, send_sem, recv_sem, device):
    return pltpu.make_async_remote_copy(
        src_ref=source,
        dst_ref=target,
        send_sem=send_sem,
        recv_sem=recv_sem,
        device_id=device,
        device_id_type=MESH,
    )


def layer_norm(hidden, gain, shift):
    mean = jnp.sum(hidden, axis=1, keepdims=True) * (1.0 / D)
    centred = hidden - mean
    var = jnp.sum(centred * centred, axis=1, keepdims=True) * (1.0 / D)
    rstd = lax.rsqrt(var + EPS)
    unit = centred * rstd
    return unit * gain + shift, unit, rstd


def layer_norm_back(grad, unit, rstd, gain):
    scaled = grad * gain
    mean_one = jnp.sum(scaled, axis=1, keepdims=True) * (1.0 / D)
    mean_two = jnp.sum(scaled * unit, axis=1, keepdims=True) * (1.0 / D)
    return rstd * (scaled - mean_one - unit * mean_two)


def fold(value):
    rows, cols = value.shape
    return jnp.sum(value.reshape(rows // 8, 8, cols), axis=0)


def column_sum(value):
    return jnp.sum(value, axis=0, keepdims=True)


SEND_SEMS, RECV_SEMS = 34, 70


def scratch_shapes(n_blk, n_wa, gather):
    n_plane, n_seq = n_wa // 2, n_blk // 2
    vmem = pltpu.VMEM
    shapes = dict(
        TOK=vmem((n_blk, 2, 2, BS, D), BF16),
        MGS=vmem((2, 32, D), BF16),
        MRS=vmem((8, 128), jnp.int32),
        MG=vmem((n_blk, 2, 32, D), BF16),
        MR=vmem((n_blk, 8, 128), jnp.int32),
        PGV=vmem((2, 8, 128), jnp.int32),
        PGS=pltpu.SMEM((2, 8, 128), jnp.int32),
        YB0=vmem((NB, BS, D), BF16),
        YB1=vmem((NB, BS, D), BF16),
        SND0=vmem((n_blk, 2, BS, D), BF16),
        SND1=vmem((n_blk, 2, BS, D), BF16),
        RET0=vmem((n_seq, 2, 2, BS, D), BF16),
        RET1=vmem((n_seq, 2, 2, BS, D), BF16),
        PSEND=vmem((4 * LAYERS, 2, HALF, D), BF16),
        PRECV=vmem((4 * LAYERS, 2, HALF, D), BF16),
        X=vmem((SEQ, D), F32),
        XL=vmem((LAYERS, SEQ, D), BF16),
        QKV=vmem((LAYERS, SEQ, 384), BF16),
        KT=vmem((LAYERS, 128, SEQ), BF16),
        VT=vmem((128, SEQ), BF16),
        PR=vmem((LAYERS, 2, SEQ, SEQ), BF16),
        AT=vmem((LAYERS, 128, SEQ), F32),
        AN=vmem((LAYERS, SEQ, 128), BF16),
        AX=vmem((LAYERS, SEQ, 128), BF16),
        ST=vmem((SEQ, HALF), F32),
        DS=vmem((2, SEQ, SEQ), BF16),
        PO=vmem((SEQ, D), F32),
        U1=vmem((LAYERS, SEQ, D), F32),
        R1=vmem((LAYERS, SEQ, 1), F32),
        U2=vmem((LAYERS, SEQ, D), F32),
        R2=vmem((LAYERS, SEQ, 1), F32),
        Y1B=vmem((LAYERS, SEQ, D), BF16),
        FS=vmem((HALF, MY_FF), F32),
        G=vmem((LAYERS, SEQ, MY_FF), BF16),
        GP=vmem((LAYERS, SEQ, MY_FF), BF16),
        DY=vmem((SEQ, D), F32),
        DD=vmem((SEQ, D), BF16),
        DF=vmem((SEQ, MY_FF), BF16),
        DH=vmem((SEQ, D), F32),
        DO=vmem((SEQ, D), BF16),
        DA=vmem((SEQ, 128), BF16),
        DAT=vmem((128, SEQ), F32),
        DQKV=vmem((SEQ, 384), BF16),
        BIAS=vmem((LAYERS, 2, NB, SEQ), F32),
        LR=vmem((2, NB, SEQ), F32),
        SGL=vmem((LAYERS, SG_ROWS, 128), F32),
        SGF=vmem((2, LAYERS, SG_ROWS, 128), F32),
        link_send=pltpu.SemaphoreType.DMA((SEND_SEMS if gather else 8,)),
        link_recv=pltpu.SemaphoreType.DMA((RECV_SEMS if gather else 12,)),
        tok_send=pltpu.SemaphoreType.DMA((3,)),
        tok_recv=pltpu.SemaphoreType.DMA((3,)),
        ret_send=pltpu.SemaphoreType.DMA((2,)),
        ret_recv=pltpu.SemaphoreType.DMA((2,)),
        local_sems=pltpu.SemaphoreType.DMA((6,)),
    )
    if gather:
        shapes.update(
            WA=vmem((LAYERS, n_blk, n_plane, 16, 512), BF16),
            WI=vmem((LAYERS, n_blk, n_plane, 16, MY_FF), BF16),
            WD=vmem((LAYERS, n_blk, n_plane, 32, D), BF16),
            WO=vmem((LAYERS, 128, D), BF16),
            WOX=vmem((LAYERS, n_blk // 2, n_plane, 16, 128), BF16),
            PV=vmem((LAYERS, PV_ROWS, 128), F32),
            LG=vmem((LAYERS, H, NB, 128), F32),
            S0=vmem((2, 16, 512), BF16),
            R0=vmem((2, 16, 512), BF16),
            SP=vmem((n_blk, n_plane, 2, 8, 128), F32),
            FX=vmem((LAYERS, 8, 1024), F32),
            RX=vmem((LAYERS, 8, 1024), F32),
            SGP=vmem((LAYERS, n_plane - 1, SG_ROWS, 128), F32),
            SGS=vmem((LAYERS, SG_ROWS, 128), F32),
            SGZ=vmem((LAYERS, n_blk - 1, SG_ROWS, 128), F32),
            BT=vmem((LAYERS, PV_ROWS, 128), F32),
        )
        for kind, (rows, cols) in RS_KINDS.items():
            shapes["G_" + kind] = vmem((LAYERS, n_blk, n_plane, rows, cols), BF16)
            shapes["RP_" + kind] = vmem((LAYERS, 2, 3, n_blk // 2, rows, cols), BF16)
            shapes["SZ_" + kind] = vmem((LAYERS, n_blk, rows, cols), BF16)
            shapes["RZ_" + kind] = vmem((LAYERS, n_blk - 1, rows, cols), BF16)
    return shapes


RS_KINDS = {"d": (32, D), "i": (16, MY_FF), "o": (16, 128), "q": (16, 384)}


def make_kernel(n_blk, n_wa, gather, in_names, out_names, scratch_names):
    n_plane = n_wa // 2
    n_seq = n_blk // 2
    n_slots = n_blk * BLK_DEV

    def kernel(*refs):
        r = dict(zip(in_names + out_names + scratch_names, refs))
        place_smem = r["place_smem"]
        z = lax.axis_index("blk")
        w = lax.axis_index("wa")
        c = lax.rem(w, 2)
        p = lax.div(w, 2)
        group = lax.div(z, n_seq)
        seq = lax.rem(z, n_seq)
        partner = (z, p * 2 + (1 - c))
        links = Links(r["link_send"], r["link_recv"], partner)
        x_peer, y_peer = (z, w ^ 2), (z, w ^ 4)
        local_sems = r["local_sems"]
        my_cols = pl.ds(pl.multiple_of(c * 128, 128), 128)
        other_cols = pl.ds(pl.multiple_of((1 - c) * 128, 128), 128)

        TOK, MGS, MRS, MG, MR = (r[name] for name in ("TOK", "MGS", "MRS", "MG", "MR"))
        PGV, PGS = r["PGV"], r["PGS"]
        PGV[c, 0:1, 0:n_slots] = r["place_vmem"][...]
        MGS[...] = r["masked_grad"][...].astype(BF16).reshape(2, 32, D)
        chosen = r["masked_pos"][...]
        slot_of = lax.shift_right_logical(chosen, 6)
        block_of = jnp.zeros_like(chosen)
        for j in range(BLK_DEV):
            block_of = jnp.where(slot_of == j, place_smem[0, z * BLK_DEV + j], block_of)
        target_row = block_of * BS + (chosen & (BS - 1))
        target_row = jnp.where(lanes(chosen.shape) < r["masked_count"][0, 0], target_row, -1)
        MRS[0:1, 0:64] = target_row
        MRS[0:1, 64:128] = target_row
        if gather:
            WA, WI, WD, SP = r["WA"], r["WI"], r["WD"], r["SP"]
            own_rows = ([], [])
            give_rows = ([], [])
            for l in range(LAYERS):
                qkv = r["w_qkv"][l].astype(F32)
                out_part = r["w_out"][l].astype(F32)
                inner = r["w_in"][l].astype(F32)
                sides = []
                for side in (0, 1):
                    at = 128 * side
                    attn = [qkv[:, 256 * j + at : 256 * j + at + 128] for j in range(3)]
                    attn = jnp.concatenate(attn + [out_part[:, at : at + 128]], axis=1)
                    feed = []
                    for t in range(4):
                        first = inner[:, 256 * t : 256 * t + 128]
                        second = inner[:, 256 * t + 128 : 256 * t + 256]
                        feed.append(pick_groups(first, second, side))
                    sides.append((attn, jnp.concatenate(feed, axis=1)))
                for kind in (0, 1):
                    own_rows[kind].append(jnp.where(c == 0, sides[0][kind], sides[1][kind]))
                    give_rows[kind].append(jnp.where(c == 0, sides[1][kind], sides[0][kind]))
                WD[l, z, p] = r["w_down"][l]
            for kind in (0, 1):
                r["S0"][kind] = jnp.concatenate(give_rows[kind], axis=0).astype(BF16)
            SP[z, p, c] = jnp.zeros((8, 128), F32)
            widths = []
            for at, name in ((0, "biases"), (2, "gains"), (4, "mask_logits")):
                part = r[name][...].astype(F32)
                widths.append(part.shape[1])
                SP[z, p, c, at : at + 2, 0 : part.shape[1]] = part

        barrier = pltpu.get_barrier_semaphore()
        greeted = 0
        for m in range(n_blk):
            for other in (0, 1):
                if m or other:
                    pl.semaphore_signal(barrier, inc=1, device_id=(z ^ m, w ^ other), device_id_type=MESH)
                    greeted += 1
        if gather:
            for m in range(1, n_plane):
                pl.semaphore_signal(barrier, inc=1, device_id=(z, w ^ (2 * m)), device_id_type=MESH)
                greeted += 1
        pl.semaphore_wait(barrier, greeted)

        place_in = links.recv_sem()
        links.push(PGV.at[c], PGV.at[c], links.send_sem(PGV.at[0]), place_in, partner)
        if gather:
            rows_in = links.recv_sem()
            links.push(r["S0"], r["R0"], links.send_sem(r["S0"]), rows_in, partner)
            small_in = links.recv_sem()
            links.push(SP.at[z, p, c], SP.at[z, p, c], links.send_sem(SP.at[0, 0, 0]), small_in, partner)

        at_home = c == group

        def move(here, source, target, send_sem, recv_sem, local_sem, device):
            @pl.when(jnp.logical_not(here))
            def _():
                remote(source, target, send_sem, recv_sem, device).start()

            @pl.when(here)
            def _():
                pltpu.make_async_copy(source, target, local_sem).start()

        def wait_pieces(pieces, count, sem, local_sem, sending):
            def wait(n):
                copy = remote(pieces(n), pieces(n), sem, sem, partner)
                if sending:
                    copy.wait_send()
                else:
                    copy.wait_recv()

            @pl.when(jnp.logical_not(at_home))
            def _():
                wait(count)

            @pl.when(at_home)
            def _():
                wait(count - 1)
                if not sending:
                    pltpu.make_async_copy(pieces(1), pieces(1), local_sem).wait()

        def token_pieces(kind):
            def pieces(n):
                return (TOK.at[pl.ds(0, n), 0], MG.at[pl.ds(0, n), 0], MR.at[pl.ds(0, n)])[kind]

            return pieces

        def send_kind(kind, sequences=range(n_seq)):
            for s in sequences:
                chip = c * n_seq + s
                for core in (0, 1):
                    here = jnp.logical_and(chip == z, c == core)
                    source = (r["tokens"].at[pl.ds(2 * core, 2)], MGS.at[core], MRS)[kind]
                    target = (TOK.at[z, core], MG.at[z, core], MR.at[z])[kind]
                    sems = (r["tok_send"].at[kind], r["tok_recv"].at[kind])
                    move(here, source, target, *sems, local_sems.at[kind], (chip, p * 2 + core))

        def take_kind(kind):
            wait_pieces(token_pieces(kind), n_blk, r["tok_recv"].at[kind], local_sems.at[kind], False)

        if gather:
            weight_refs = (WA, WI, WD)
            ag_recv = {}
            ag_send = {}
            for kind in (0, 1, 2):
                ref = weight_refs[kind]
                likes = (ref.at[:, 0, 0:3], ref.at[0], ref.at[0, 0:2])
                ag_send[kind] = [links.send_sem(like) for like in likes]
            ag_send["small"] = [links.send_sem(like) for like in (SP.at[0, 0:3], SP.at[:, 0:2], SP.at[0:2, 0:2])]

            def rows_at(name, z_at, p_at):
                if name == "small":
                    return SP.at[z_at, p_at]
                return weight_refs[name[0]].at[name[1], z_at, p_at]

            def ag_push(name, stage, z_at, p_at, device):
                ref = rows_at(name, z_at, p_at)
                send_sem = ag_send[name if name == "small" else name[0]][stage]
                links.push(ref, ref, send_sem, ag_recv[name][stage], device)

            every, z_low, z_high = slice(0, 4), slice(0, 2), slice(2, 4)

            def ag_z(name):
                ag_recv[name] = [links.recv_sem() for _ in range(3)]
                for m in range(1, n_blk):
                    ag_push(name, 0, z, p, (z ^ m, w))

            def ag_xy(name):
                links.arrived(rows_at(name, 0, slice(0, 3)), ag_recv[name][0])
                ag_push(name, 1, every, p, x_peer)
                ag_push(name, 1, every, p, y_peer)

            def ag_pass(name):
                links.arrived(rows_at(name, every, z_low), ag_recv[name][1])
                ag_push(name, 2, z_low, p ^ 1, y_peer)
                ag_push(name, 2, z_high, p ^ 2, x_peer)

            def ag_ready(name):
                links.arrived(rows_at(name, z_low, z_low), ag_recv[name][2])

            def merge_rows(kind, l):
                own = own_rows[kind][l]
                other = r["R0"][kind].astype(F32)[8 * l : 8 * l + 8]
                merged = jnp.concatenate([jnp.where(c == 0, own, other), jnp.where(c == 0, other, own)], axis=0)
                weight_refs[kind][l, z, p] = merged.astype(BF16)

        if gather:
            links.arrived(r["R0"], rows_in)
            merge_rows(0, 0)
            ag_z((0, 0))
            links.arrived(SP.at[0, 0, 0], small_in)
            ag_z("small")
            merge_rows(1, 0)
            ag_z((1, 0))
            ag_z((2, 0))
        send_kind(0)
        if gather:
            merge_rows(0, 1)
            merge_rows(1, 1)
            ag_xy((0, 0))
            ag_xy("small")
            ag_xy((1, 0))
            ag_xy((2, 0))
            ag_z((0, 1))
            ag_pass((0, 0))
            ag_pass("small")
            ag_z((1, 1))
            ag_z((2, 1))
            ag_pass((1, 0))
            ag_pass((2, 0))

        take_kind(0)
        tokens_in = links.recv_sem()
        links.push(TOK.at[:, c], TOK.at[:, c], links.send_sem(TOK.at[:, 0]), tokens_in, partner)
        if gather:
            ag_xy((0, 1))
        links.arrived(PGV.at[0], place_in)
        to_scalars = pltpu.make_async_copy(PGV, PGS, local_sems.at[3])
        to_scalars.start()
        to_scalars.wait()
        links.arrived(TOK.at[:, 0], tokens_in)
        X, XL = r["X"], r["XL"]
        for b in range(NB):
            at = jnp.int32(0)
            for j in range(n_slots):
                at = jnp.where(PGS[group, 0, j] == seq * NB + b, j, at)
            block = TOK[lax.div(at, 4), lax.rem(lax.div(at, 2), 2), lax.rem(at, 2)]
            X[b * BS : (b + 1) * BS] = block.astype(F32)
            XL[0, b * BS : (b + 1) * BS] = block

        send_kind(1)
        send_kind(2)

        PV, LG = r["PV"], r["LG"]
        if gather:
            ag_ready("small")
            lane = lanes((1, 128))
            for l in range(LAYERS):
                for first_row, count, width, kind_row in ((0, 20, widths[0], 0), (20, 4, widths[1], 2)):
                    tiles = [jnp.zeros((1, 128), F32)] * count
                    for device in range(n_blk * n_wa):
                        t, offset = divmod(device * width, 128)
                        dz, dw = divmod(device, n_wa)
                        piece = SP[dz, dw // 2, dw % 2, kind_row + l : kind_row + l + 1, :]
                        if offset:
                            piece = turn(piece, offset)
                        if offset + width <= 128:
                            tiles[t] = tiles[t] + piece
                        else:
                            tiles[t] = tiles[t] + jnp.where(lane >= offset, piece, 0.0)
                            tiles[t + 1] = tiles[t + 1] + jnp.where(lane < offset, piece, 0.0)
                    for t in range(count):
                        PV[l, first_row + t : first_row + t + 1, :] = tiles[t]
                for h in range(H):
                    for i in range(NB):
                        LG[l, h, i : i + 1, :] = SP[h, i // 2, i % 2, 4 + l : 5 + l, :]

        def wide(l, row):
            return jnp.concatenate([PV[l, row : row + 1, :], PV[l, row + 1 : row + 2, :]], axis=1)

        def mine(l, row):
            return jnp.where(c == 0, PV[l, row : row + 1, :], PV[l, row + 1 : row + 2, :])

        BIAS = r["BIAS"]
        spread = lax.broadcasted_iota(jnp.int32, (16, SEQ), 1) // BS
        spread = (spread == lax.broadcasted_iota(jnp.int32, (16, SEQ), 0)).astype(F32).astype(BF16)

        def over_rows(table):
            table = jnp.concatenate([table, jnp.zeros_like(table)], axis=0).astype(BF16)
            return tn(table, spread)[0:NB]

        for h in (0, 1):
            allowed = over_rows(r["block_mask"][2 * c + h].astype(F32)) > 0.5
            for l in range(LAYERS):
                logit = over_rows(LG[l, 2 * c + h])
                log_sig = jnp.minimum(logit, 0.0) - jnp.log1p(jnp.exp(-jnp.abs(logit)))
                BIAS[l, h] = jnp.where(allowed, log_sig, NEG)

        PSEND, PRECV = r["PSEND"], r["PRECV"]
        exchange_out = links.send_sem(PSEND)
        exchange_in = [links.recv_sem() for _ in range(4)]

        def give(step, chunk, value):
            PSEND[step, chunk] = value.astype(BF16)
            sem = exchange_in[2 * (step % 2) + chunk]
            links.push(PSEND.at[step, chunk], PRECV.at[step, chunk], exchange_out, sem, partner)

        def take(step, chunk):
            links.arrived(PRECV.at[step, chunk], exchange_in[2 * (step % 2) + chunk])

        def of_head(value, h):
            keep = (lanes(value.shape) // HD) == h
            return jnp.where(keep, value, jnp.zeros_like(value))

        def rows_of(chunk):
            return slice(chunk * HALF, (chunk + 1) * HALF)

        YB, SND, RET = ((r[name + "0"], r[name + "1"]) for name in ("YB", "SND", "RET"))

        def send_back(which):
            for dest in range(n_blk):
                for j in range(2):
                    position = lax.rem(PGS[group, 0, dest * BLK_DEV + 2 * c + j], NB)
                    SND[which][dest, j] = YB[which][position]
                here = jnp.logical_and(dest == z, c == group)
                sems = (r["ret_send"].at[which], r["ret_recv"].at[which])
                target = RET[which].at[seq, c]
                move(here, SND[which].at[dest], target, *sems, local_sems.at[4 + which], (dest, p * 2 + group))

        def return_pieces(which):
            return lambda n: SND[which].at[pl.ds(0, n)]

        def take_back(which, target_ref):
            wait_pieces(return_pieces(which), 2 * n_seq, r["ret_recv"].at[which], local_sems.at[4 + which], False)
            for j in range(BLK_DEV):
                from_seq = lax.div(place_smem[0, z * BLK_DEV + j], NB)
                target_ref[j] = RET[which][from_seq, j // 2, j % 2].astype(F32)

        QKV, KT, VT, PR, AT, AN, AX = (r[n] for n in ("QKV", "KT", "VT", "PR", "AT", "AN", "AX"))
        ST, DS, PO, FS, G, GP, Y1B = (r[n] for n in ("ST", "DS", "PO", "FS", "G", "GP", "Y1B"))
        U1, R1, U2, R2 = (r[n] for n in ("U1", "R1", "U2", "R2"))
        WO = r["WO"]
        attended_out, attended_in = links.send_sem(AX), links.recv_sem()
        if gather:
            wo_out = links.send_sem(r["WOX"])

        def weight(kind, l):
            if gather:
                ref = weight_refs[kind]
                return ref[l].reshape(ref.shape[1] * ref.shape[2] * ref.shape[3], ref.shape[4])
            return (r["WA"], r["WI"], r["WD"])[kind][l]

        def weight_qkv(l):
            if gather:
                return WA[l, :, :, :, 0:384].reshape(D, 384)
            return r["WA"][l, :, 0:384]

        for l in range(LAYERS):
            step = 2 * l
            if gather:
                ag_ready((0, l))
                part = n_blk // 2
                wo_in = links.recv_sem()
                theirs = WA.at[l, pl.ds((1 - c) * part, part), :, :, pl.ds(384, 128)]
                links.push(theirs, r["WOX"].at[l], wo_out, wo_in, partner)
                WO[l, :, my_cols] = WA[l, pl.ds(c * part, part), :, :, 384:512].reshape(128, 128)
            bias = jnp.concatenate([mine(l, ROW_BQ), jnp.zeros((1, 128), F32), mine(l, ROW_BV)], axis=1)
            scale = jnp.where(lanes((1, 384)) < 128, 0.125, 1.0)
            for chunk in range(2):
                rows = rows_of(chunk)
                QKV[l, rows] = ((nn(XL[l, rows], weight_qkv(l)) + bias) * scale).astype(BF16)
            keys = QKV[l, :, 128:256]
            KT[l] = keys.astype(F32).T.astype(BF16)
            VT[...] = QKV[l, :, 256:384].astype(F32).T.astype(BF16)
            if gather:
                if l + 1 < LAYERS:
                    ag_xy((1, l + 1))
                    ag_xy((2, l + 1))
                links.arrived(r["WOX"].at[l], wo_in)
                WO[l, :, other_cols] = r["WOX"][l].reshape(128, 128)
            for chunk in range(2):
                rows = rows_of(chunk)
                for h in (0, 1):
                    queries = of_head(QKV[l, rows, 0:128], h)
                    ST[...] = nt(keys, queries)
                    top = jnp.full((8, HALF), NEG, F32)
                    for kb in range(NB):
                        score = ST[kb * BS : (kb + 1) * BS] + BIAS[l, h, kb : kb + 1, rows]
                        top = jnp.maximum(top, jnp.max(score.reshape(8, 8, HALF), axis=0))
                    top = jnp.max(top, axis=0, keepdims=True)
                    total = jnp.zeros((8, HALF), F32)
                    for kb in range(NB):
                        score = ST[kb * BS : (kb + 1) * BS] + BIAS[l, h, kb : kb + 1, rows]
                        weight_of = jnp.exp(score - top)
                        ST[kb * BS : (kb + 1) * BS] = weight_of
                        total = total + fold(weight_of)
                    inverse = 1.0 / column_sum(total)
                    for kb in range(NB):
                        PR[l, h, kb * BS : (kb + 1) * BS, rows] = (ST[kb * BS : (kb + 1) * BS] * inverse).astype(BF16)
                    AT[l, h * HD : (h + 1) * HD, rows] = nn(VT[h * HD : (h + 1) * HD], PR[l, h, :, rows])
                AN[l, rows] = AT[l, :, rows].T.astype(BF16)
                branch = nn(AN[l, rows], WO[l])
                give(step, chunk, branch)
                PO[rows] = X[rows] + branch + wide(l, ROW_BO)
                part = pl.ds(chunk * HALF, HALF)
                links.push(AN.at[l, part], AX.at[l, part], attended_out, attended_in, partner)
            if gather:
                if l + 1 < LAYERS:
                    ag_pass((0, l + 1))
                    ag_pass((1, l + 1))
                    ag_pass((2, l + 1))
                ag_ready((1, l))
                ag_ready((2, l))
            for chunk in range(2):
                rows = rows_of(chunk)
                take(step, chunk)
                gain, shift = wide(l, ROW_G1), wide(l, ROW_S1)
                for t in range(0, HALF, BS):
                    tile = slice(chunk * HALF + t, chunk * HALF + t + BS)
                    hidden = PO[tile] + PRECV[step, chunk, t : t + BS].astype(F32)
                    normed, unit, rstd = layer_norm(hidden, gain, shift)
                    U1[l, tile] = unit
                    R1[l, tile] = rstd
                    X[tile] = normed
                    Y1B[l, tile] = normed.astype(BF16)
                FS[...] = nn(Y1B[l, rows], weight(1, l))
                inner_bias = []
                for t in range(4):
                    row = ROW_BI + 2 * t
                    inner_bias.append(pick_groups(PV[l, row : row + 1, :], PV[l, row + 1 : row + 2, :], c))
                inner_bias = jnp.concatenate(inner_bias, axis=1)
                for t in range(0, HALF, 32):
                    tile = slice(chunk * HALF + t, chunk * HALF + t + 32)
                    inner = FS[t : t + 32] + inner_bias
                    below = 0.5 + 0.5 * lax.erf(inner * 0.7071067811865476)
                    G[l, tile] = (inner * below).astype(BF16)
                    slope = below + inner * (jnp.exp(inner * inner * -0.5) * 0.3989422804014327)
                    GP[l, tile] = slope.astype(BF16)
                branch = nn(G[l, rows], weight(2, l))
                give(step + 1, chunk, branch)
                PO[rows] = X[rows] + branch + wide(l, ROW_BD)
            for chunk in range(2):
                take(step + 1, chunk)
                gain, shift = wide(l, ROW_G2), wide(l, ROW_S2)
                for t in range(0, HALF, BS):
                    tile = slice(chunk * HALF + t, chunk * HALF + t + BS)
                    hidden = PO[tile] + PRECV[step + 1, chunk, t : t + BS].astype(F32)
                    normed, unit, rstd = layer_norm(hidden, gain, shift)
                    U2[l, tile] = unit
                    R2[l, tile] = rstd
                    X[tile] = normed
                    if l + 1 < LAYERS:
                        XL[l + 1, tile] = normed.astype(BF16)
                    else:
                        YB[0][chunk * 4 + t // BS] = normed.astype(BF16)
        send_back(0)

        DY, DD, DF, DH, DO, DA, DAT, DQKV = (r[n] for n in ("DY", "DD", "DF", "DH", "DO", "DA", "DAT", "DQKV"))
        LR, SGL = r["LR"], r["SGL"]
        take_kind(1)
        take_kind(2)
        grads_in = links.recv_sem()
        links.push(MG.at[:, c], MG.at[:, c], links.send_sem(MG.at[:, 0]), grads_in, partner)
        links.arrived(MG.at[:, 0], grads_in)
        wanted = []
        lane = lanes((1, 128))
        for t in range(n_blk // 2):
            wanted.append(jnp.where(lane < 64, MR[2 * t, 0:1, :], MR[2 * t + 1, 0:1, :]))
        wanted = jnp.concatenate(wanted, axis=1) - seq * SEQ
        listed = MG[...].reshape(n_blk * 64, D)
        for chunk in range(2):
            row_ids = lax.broadcasted_iota(jnp.int32, (HALF, n_blk * 64), 0) + chunk * HALF
            DY[rows_of(chunk)] = nn((row_ids == wanted).astype(F32).astype(BF16), listed)

        rs_recv = {}
        if gather:
            rs_out = {kind: (links.send_sem(r["RP_" + kind]), links.send_sem(r["RZ_" + kind])) for kind in RS_KINDS}

        def rs_start(kind, l):
            if not gather:
                return
            rs_recv[kind, l] = [links.recv_sem() for _ in range(3)]
            grad, parts, sem = r["G_" + kind], r["RP_" + kind], rs_recv[kind, l][0]
            out = rs_out[kind][0]
            links.push(grad.at[l, z_low, p ^ 3], parts.at[l, 0, 1], out, sem, x_peer)
            links.push(grad.at[l, z_high, p ^ 3], parts.at[l, 1, 1], out, sem, y_peer)
            links.push(grad.at[l, z_low, p ^ 1], parts.at[l, 0, 0], out, sem, x_peer)
            links.push(grad.at[l, z_high, p ^ 2], parts.at[l, 1, 0], out, sem, y_peer)

        def rs_pass(kind, l):
            if not gather:
                return
            grad, parts, sem = r["G_" + kind], r["RP_" + kind], rs_recv[kind, l][1]
            links.arrived(parts.at[l, :, 0:2], rs_recv[kind, l][0])
            parts[l, 0, 1] = (grad[l, z_low, p ^ 2].astype(F32) + parts[l, 0, 1].astype(F32)).astype(BF16)
            links.push(parts.at[l, 0, 1], parts.at[l, 1, 2], rs_out[kind][0], sem, y_peer)
            parts[l, 1, 1] = (grad[l, z_high, p ^ 1].astype(F32) + parts[l, 1, 1].astype(F32)).astype(BF16)
            links.push(parts.at[l, 1, 1], parts.at[l, 0, 2], rs_out[kind][0], sem, x_peer)

        def rs_z(kind, l):
            if not gather:
                return
            grad, parts, total = r["G_" + kind], r["RP_" + kind], r["SZ_" + kind]
            links.arrived(parts.at[l, :, 2], rs_recv[kind, l][1])
            for half, straight, passed in ((z_low, 0, 1), (z_high, 1, 0)):
                value = grad[l, half, p].astype(F32) + parts[l, straight, 0].astype(F32) + parts[l, passed, 2].astype(F32)
                total[l, half] = value.astype(BF16)
            for m in range(1, n_blk):
                links.push(total.at[l, z ^ m], r["RZ_" + kind].at[l, m - 1], rs_out[kind][1], rs_recv[kind, l][2], (z ^ m, w))

        def rs_end(kind, l):
            total = r["SZ_" + kind][l, z].astype(F32)
            links.arrived(r["RZ_" + kind].at[l], rs_recv[kind, l][2])
            for m in range(1, n_blk):
                total = total + r["RZ_" + kind][l, m - 1].astype(F32)
            return total

        sg_recv = {}
        if gather:
            sg_out = (links.send_sem(r["SGP"]), links.send_sem(r["SGZ"]))

        def small_start(l):
            if not gather:
                return
            sg_recv[l] = [links.recv_sem() for _ in range(2)]
            for m in range(1, n_plane):
                links.push(SGL.at[l], r["SGP"].at[l, m - 1], sg_out[0], sg_recv[l][0], (z, w ^ (2 * m)))

        def small_z(l):
            if not gather:
                return
            links.arrived(r["SGP"].at[l], sg_recv[l][0])
            total = SGL[l]
            for m in range(1, n_plane):
                total = total + r["SGP"][l, m - 1]
            r["SGS"][l] = total
            for m in range(1, n_blk):
                links.push(r["SGS"].at[l], r["SGZ"].at[l, m - 1], sg_out[1], sg_recv[l][1], (z ^ m, w))

        def small_end(l):
            links.arrived(r["SGZ"].at[l], sg_recv[l][1])
            total = r["SGS"][l]
            for m in range(1, n_blk):
                total = total + r["SGZ"][l, m - 1]
            return total

        def store_grad(kind, l, value):
            if gather:
                shape = r["G_" + kind].shape
                r["G_" + kind][l] = value.astype(BF16).reshape(shape[1:])
            else:
                r["G_" + kind][l] = value

        def two_rows(l, row, value):
            SGL[l, row : row + 1, :] = value[:, 0:128]
            SGL[l, row + 1 : row + 2, :] = value[:, 128:256]

        SGL[...] = jnp.zeros_like(SGL)
        for l in reversed(range(LAYERS)):
            step = 4 + 2 * (LAYERS - 1 - l)
            gain = wide(l, ROW_G2)
            sums = [jnp.zeros((8, D), F32) for _ in range(3)]
            inner_sum = jnp.zeros((8, MY_FF), F32)
            for chunk in range(2):
                rows = rows_of(chunk)
                for t in range(0, HALF, BS):
                    tile = slice(chunk * HALF + t, chunk * HALF + t + BS)
                    grad, unit = DY[tile], U2[l, tile]
                    if l < LAYERS - 1:
                        if t == 0:
                            take(step - 1, chunk)
                        grad = grad + PRECV[step - 1, chunk, t : t + BS].astype(F32)
                    d_hidden = layer_norm_back(grad, unit, R2[l, tile], gain)
                    low = d_hidden.astype(BF16)
                    DH[tile] = d_hidden
                    DD[tile] = low
                    sums[0] = sums[0] + fold(grad * unit)
                    sums[1] = sums[1] + fold(grad)
                    sums[2] = sums[2] + fold(low.astype(F32))
                FS[...] = nt(DD[rows], weight(2, l))
                for t in range(0, HALF, 32):
                    tile = slice(chunk * HALF + t, chunk * HALF + t + 32)
                    d_inner = (FS[t : t + 32] * GP[l, tile].astype(F32)).astype(BF16)
                    DF[tile] = d_inner
                    inner_sum = inner_sum + fold(d_inner.astype(F32))
                branch = nt(DF[rows], weight(1, l))
                give(step, chunk, branch)
                DH[rows] = DH[rows] + branch
            two_rows(l, SG_G2, column_sum(sums[0]))
            two_rows(l, SG_S2, column_sum(sums[1]))
            two_rows(l, SG_BD, column_sum(sums[2]))
            inner_sum = column_sum(inner_sum)
            for t in range(4):
                SGL[l, SG_BI + t : SG_BI + t + 1, :] = inner_sum[:, 128 * t : 128 * t + 128]
            store_grad("d", l, tn(G[l], DD[...]))
            rs_start("d", l)
            store_grad("i", l, tn(Y1B[l], DF[...]))
            rs_start("i", l)
            if l < LAYERS - 1:
                rs_pass("q", l + 1)
                rs_z("d", l + 1)
            gain = wide(l, ROW_G1)
            sums = [jnp.zeros((8, D), F32) for _ in range(3)]
            for chunk in range(2):
                rows = rows_of(chunk)
                take(step, chunk)
                for t in range(0, HALF, BS):
                    tile = slice(chunk * HALF + t, chunk * HALF + t + BS)
                    grad = DH[tile] + PRECV[step, chunk, t : t + BS].astype(F32)
                    unit = U1[l, tile]
                    d_hidden = layer_norm_back(grad, unit, R1[l, tile], gain)
                    low = d_hidden.astype(BF16)
                    DH[tile] = d_hidden
                    DO[tile] = low
                    sums[0] = sums[0] + fold(grad * unit)
                    sums[1] = sums[1] + fold(grad)
                    sums[2] = sums[2] + fold(low.astype(F32))
                DA[rows] = nt(DO[rows], WO[l]).astype(BF16)
                DAT[:, rows] = nt(WO[l], DO[rows]).astype(BF16).astype(F32)
            two_rows(l, SG_G1, column_sum(sums[0]))
            two_rows(l, SG_S1, column_sum(sums[1]))
            two_rows(l, SG_BO, column_sum(sums[2]))
            if l == LAYERS - 1:
                links.arrived(AX, attended_in)
            own_part = tn(AN[l], DO[:, my_cols])
            other_part = tn(AX[l], DO[:, my_cols])
            if gather:
                part = n_blk // 2
                shape = (part, n_plane, 16, 128)
                r["G_o"][l, pl.ds(c * part, part)] = own_part.astype(BF16).reshape(shape)
                r["G_o"][l, pl.ds((1 - c) * part, part)] = other_part.astype(BF16).reshape(shape)
            else:
                r["G_o"][l, c] = own_part
                r["G_o"][l, 1 - c] = other_part
            rs_start("o", l)
            if l < LAYERS - 1:
                rs_z("i", l + 1)
                small_z(l + 1)
            keys, values = QKV[l, :, 128:256], QKV[l, :, 256:384]
            for chunk in range(2):
                rows = rows_of(chunk)
                d_query = []
                for h in (0, 1):
                    head = slice(h * HD, (h + 1) * HD)
                    ST[...] = nt(values, of_head(DA[rows], h))
                    inner = column_sum(DAT[head, rows] * AT[l, head, rows])
                    for kb in range(NB):
                        block = slice(kb * BS, (kb + 1) * BS)
                        d_score = PR[l, h, block, rows].astype(F32) * (ST[block] - inner)
                        DS[h, block, rows] = d_score.astype(BF16)
                        LR[h, kb : kb + 1, rows] = column_sum(fold(d_score))
                    d_query.append(nn(KT[l, head], DS[h, :, rows]))
                d_query = jnp.concatenate(d_query, axis=0) * 0.125
                DQKV[rows, 0:128] = d_query.T.astype(BF16)
                if l == LAYERS - 1:
                    if chunk == 1:
                        rs_pass("d", l)
                else:
                    rs_z("oq"[chunk], l + 1)
                    rs_pass("di"[chunk], l)
            d_keys = jnp.zeros((SEQ, 128), F32)
            d_values = jnp.zeros((SEQ, 128), F32)
            for h in (0, 1):
                d_keys = d_keys + nn(DS[h], of_head(QKV[l, :, 0:128], h))
                d_values = d_values + nn(PR[l, h], of_head(DA[...], h))
            DQKV[:, 128:256] = d_keys.astype(BF16)
            DQKV[:, 256:384] = d_values.astype(BF16)
            by_block = lax.broadcasted_iota(jnp.int32, (128, SEQ), 1) // BS
            by_block = (by_block == lax.broadcasted_iota(jnp.int32, (128, SEQ), 0)).astype(F32)
            for h in (0, 1):
                table = lax.dot_general(
                    LR[h], by_block, (((1,), (1,)), ((), ())), preferred_element_type=F32, precision=HIGHEST
                )
                SGL[l, SG_LG + 8 * h : SG_LG + 8 * h + 8, :] = table
            for chunk in range(2):
                rows = rows_of(chunk)
                branch = nt(DQKV[rows], weight_qkv(l))
                give(step + 1, chunk, branch)
                DY[rows] = DH[rows] + branch
            store_grad("q", l, tn(XL[l], DQKV[...]))
            rs_start("q", l)
            SGL[l, SG_BQ : SG_BQ + 1, :] = column_sum(fold(DQKV[:, 0:128].astype(F32)))
            SGL[l, SG_BV : SG_BV + 1, :] = column_sum(fold(DQKV[:, 256:384].astype(F32)))
            small_start(l)
            if l == LAYERS - 1:
                rs_pass("i", l)
            rs_pass("o", l)
        for chunk in range(2):
            take(step + 1, chunk)
            for t in range(0, HALF, BS):
                tile = slice(chunk * HALF + t, chunk * HALF + t + BS)
                grad = DY[tile] + PRECV[step + 1, chunk, t : t + BS].astype(F32)
                YB[1][chunk * 4 + t // BS] = grad.astype(BF16)
        send_back(1)
        SGF = r["SGF"]
        if gather:
            rs_z("d", 0)
            rs_z("i", 0)
            rs_pass("q", 0)
            rs_z("o", 0)
            small_z(0)
            FX, RX = r["FX"], r["RX"]
            kept = {}

            def finish(kind, l, at):
                total = rs_end(kind, l)
                width = total.shape[1]
                kept[kind, l] = jnp.where(c == 0, total[0:8], total[8:16])
                FX[l, :, at : at + width] = jnp.where(c == 0, total[8:16], total[0:8])

            for l in reversed(range(LAYERS)):
                r["gdown"][l] = rs_end("d", l)
                finish("i", l, 512)
                if l > 0:
                    finish("o", l, 384)
                    finish("q", l, 0)
                    SGF[c, l] = small_end(l)
                if l == LAYERS - 1:
                    rs_z("q", 0)
        take_back(0, r["out"])
        if gather:
            finish("o", 0, 384)
            SGF[c, 0] = small_end(0)
            sgf_in = links.recv_sem()
            links.push(SGF.at[c], SGF.at[c], links.send_sem(SGF.at[0]), sgf_in, partner)
            finish("q", 0, 0)
            fx_in = links.recv_sem()
            links.push(FX, RX, links.send_sem(FX), fx_in, partner)
            links.arrived(SGF.at[0], sgf_in)
        else:
            SGF[c] = SGL[...]
            SGF[1 - c] = jnp.zeros(SGL.shape, F32)
        for l in range(LAYERS):

            def put(at, value):
                if gather:
                    r["BT"][l, at : at + 1, :] = value
                elif at < ROW_G1:
                    r["gbias"][l : l + 1, 128 * at : 128 * at + 128] = value
                else:
                    at -= ROW_G1
                    r["ggain"][l : l + 1, 128 * at : 128 * at + 128] = value

            def row(core, at):
                return SGF[core, l, at : at + 1, :]

            for core in (0, 1):
                put(ROW_BQ + core, row(core, SG_BQ))
                put(ROW_BV + core, row(core, SG_BV))
                if not gather:
                    for h in (0, 1):
                        r["glog"][l, 2 * core + h] = SGF[core, l, SG_LG + 8 * h : SG_LG + 8 * h + 8, :]
            singles = ((ROW_BO, SG_BO), (ROW_S1, SG_S1), (ROW_BD, SG_BD), (ROW_S2, SG_S2), (ROW_G1, SG_G1), (ROW_G2, SG_G2))
            for at, source in singles:
                for j in (0, 1):
                    put(at + j, row(0, source + j))
            for t in range(4):
                first, second = weave_groups(row(0, SG_BI + t), row(1, SG_BI + t))
                put(ROW_BI + 2 * t, first)
                put(ROW_BI + 2 * t + 1, second)
            if gather:
                index = z * n_wa + w
                lane = lanes((1, 128))

                def entries(first_row, width):
                    start = index * width
                    tile, offset = lax.div(start, 128), lax.rem(start, 128)
                    shift = lax.rem(128 - offset, 128)
                    first = pltpu.roll(r["BT"][l, pl.ds(first_row + tile, 1), :], shift, 1)
                    if 128 % width == 0:
                        return first[:, 0:width]
                    second = pltpu.roll(r["BT"][l, pl.ds(first_row + tile + 1, 1), :], shift, 1)
                    return jnp.where(lane < 128 - offset, first, second)[:, 0:width]

                r["gbias"][l : l + 1, :] = entries(0, widths[0])
                r["ggain"][l : l + 1, :] = entries(ROW_G1, widths[1])
                table = SGF[lax.div(z, 2), l, pl.ds(SG_LG + 8 * lax.rem(z, 2), 8), :]
                wide_lane = lanes((8, 128))
                column = jnp.sum(jnp.where(wide_lane == w, table, 0.0), axis=1, keepdims=True)
                diagonal = wide_lane == lax.broadcasted_iota(jnp.int32, (8, 128), 0)
                values_row = column_sum(jnp.where(diagonal, column, 0.0))[:, 0:NB]
                logit = r["mask_logits"][...].astype(F32)[l : l + 1]
                r["glog"][l : l + 1, :] = values_row / (1.0 + jnp.exp(logit))
        if gather:
            links.arrived(RX, fx_in)
            for l in range(LAYERS):
                own = jnp.concatenate([kept[kind, l] for kind in ("q", "o", "i")], axis=1)
                other = RX[l]
                zero = jnp.where(c == 0, own, other)
                one = jnp.where(c == 0, other, own)
                for j in range(3):
                    r["gqkv"][l, :, 256 * j : 256 * j + 128] = zero[:, 128 * j : 128 * j + 128]
                    r["gqkv"][l, :, 256 * j + 128 : 256 * j + 256] = one[:, 128 * j : 128 * j + 128]
                r["gout"][l, :, 0:128] = zero[:, 384:512]
                r["gout"][l, :, 128:256] = one[:, 384:512]
                for t in range(4):
                    at = 512 + 128 * t
                    first, second = weave_groups(zero[:, at : at + 128], one[:, at : at + 128])
                    r["gin"][l, :, 256 * t : 256 * t + 128] = first
                    r["gin"][l, :, 256 * t + 128 : 256 * t + 256] = second
        take_back(1, r["gtok"])
        links.drain()
        for kind in range(3):
            wait_pieces(token_pieces(kind), 2 * n_seq, r["tok_send"].at[kind], None, True)
        for which in range(2):
            wait_pieces(return_pieces(which), n_blk, r["ret_send"].at[which], None, True)

    return kernel


def call_kernel(n_blk, n_wa, gather, named):
    vmem = pl.BlockSpec(memory_space=pltpu.VMEM)
    smem = pl.BlockSpec(memory_space=pltpu.SMEM)
    in_names = list(named)
    shapes = dict(out=(BLK_DEV, BS, D), gtok=(BLK_DEV, BS, D))
    if gather:
        sources = ("w_qkv", "w_out", "w_in", "w_down", "biases", "gains", "mask_logits")
        results = ("gqkv", "gout", "gin", "gdown", "gbias", "ggain", "glog")
        shapes.update({result: named[source].shape for result, source in zip(results, sources)})
    else:
        shapes.update(
            gbias=(LAYERS, 6 * D + FF),
            ggain=(LAYERS, 2 * D),
            glog=(LAYERS, H, NB, 128),
            G_d=(LAYERS, MY_FF, D),
            G_i=(LAYERS, D, MY_FF),
            G_o=(LAYERS, 2, 128, 128),
            G_q=(LAYERS, D, 384),
        )
    hold = pltpu.VMEM if gather else jax.ShapeDtypeStruct
    scratch = scratch_shapes(n_blk, n_wa, gather)
    kernel = make_kernel(n_blk, n_wa, gather, in_names, list(shapes), list(scratch))
    results = pl.pallas_call(
        kernel,
        out_shape=[hold(shape, F32) for shape in shapes.values()],
        in_specs=[smem if name in ("place_smem", "masked_count") else vmem for name in in_names],
        out_specs=[vmem] * len(shapes),
        scratch_shapes=list(scratch.values()),
        compiler_params=pltpu.CompilerParams(
            collective_id=0, has_side_effects=True, vmem_limit_bytes=60 * 2**20
        ),
        name="encoder",
    )(*named.values())
    if gather:
        results = pl.pallas_call(
            write_out,
            out_shape=[jax.ShapeDtypeStruct(shape, F32) for shape in shapes.values()],
            in_specs=[vmem] * len(shapes),
            out_specs=[pl.BlockSpec(memory_space=pl.ANY)] * len(shapes),
            scratch_shapes=[pltpu.SemaphoreType.DMA((len(shapes),))],
            name="write_out",
        )(*[pltpu.with_memory_space_constraint(result, pltpu.VMEM) for result in results])
    return dict(zip(shapes, results))


def write_out(*refs):
    count = (len(refs) - 1) // 2
    sems = refs[-1]
    copies = [pltpu.make_async_copy(refs[k], refs[count + k], sems.at[k]) for k in range(count)]
    for copy in copies:
        copy.start()
    for copy in copies:
        copy.wait()


def local(
    tokens,
    placement,
    block_mask,
    w_qkv,
    w_out,
    w_in,
    w_down,
    biases,
    gains,
    mask_logits,
    masked_pos,
    masked_count,
    masked_grad,
):
    n_blk, n_wa = lax.axis_size("blk"), lax.axis_size("wa")
    both = ("blk", "wa")
    core = lax.rem(lax.axis_index("wa"), 2)
    gather = w_qkv.shape[1] == 8 and n_blk == H and n_wa == NB
    named = dict(
        tokens=tokens.reshape(BLK_DEV, BS, D),
        place_smem=placement,
        place_vmem=placement,
        block_mask=block_mask,
        masked_pos=masked_pos.reshape(1, -1),
        masked_count=masked_count,
        masked_grad=masked_grad.reshape(-1, D),
    )
    if gather:
        named.update(
            w_qkv=w_qkv, w_out=w_out, w_in=w_in, w_down=w_down, biases=biases, gains=gains, mask_logits=mask_logits
        )
    else:
        shards = (w_qkv, w_out, w_in, w_down, biases, gains, mask_logits)
        whole = [lax.all_gather(shard, both, axis=1, tiled=True) for shard in shards]
        qkv = lax.dynamic_index_in_dim(whole[0].reshape(LAYERS, D, 3, 2, 128), core, 3, False)
        qkv = qkv.reshape(LAYERS, D, 384)
        inner = lax.dynamic_index_in_dim(whole[2].reshape(LAYERS, D, 16, 2, 32), core, 3, False)
        down = lax.dynamic_index_in_dim(whole[3].reshape(LAYERS, 16, 2, 32, D), core, 2, False)
        vectors = jnp.concatenate([whole[4], whole[5]], axis=1).astype(F32)
        logits = whole[6].astype(F32).reshape(LAYERS, H, NB, NB)
        named.update(
            WA=qkv,
            WO=lax.dynamic_slice_in_dim(whole[1], core * 128, 128, axis=1),
            WI=inner.reshape(LAYERS, D, MY_FF),
            WD=down.reshape(LAYERS, MY_FF, D),
            PV=vectors.reshape(LAYERS, PV_ROWS, 128),
            LG=jnp.pad(logits, ((0, 0), (0, 0), (0, 0), (0, 128 - NB))),
        )
    got = call_kernel(n_blk, n_wa, gather, named)
    if gather:
        weight_grads = (got["gqkv"], got["gout"], got["gin"], got["gdown"])
        small = (got["gbias"], got["ggain"], got["glog"])
    else:
        grad_logits = jnp.swapaxes(got["glog"][..., 0:NB], 2, 3).reshape(LAYERS, H * NB * NB)

        def one_core(part, axis):
            halves = [jnp.where(core == side, part, 0.0) for side in (0, 1)]
            return jnp.stack(halves, axis=axis)

        whole = (
            one_core(got["G_q"].reshape(LAYERS, D, 3, 128), 3).reshape(LAYERS, D, 3 * D),
            one_core(got["G_o"].reshape(LAYERS, D, 128), 2).reshape(LAYERS, D, D),
            one_core(got["G_i"].reshape(LAYERS, D, 16, 32), 3).reshape(LAYERS, D, FF),
            one_core(got["G_d"].reshape(LAYERS, 16, 32, D), 2).reshape(LAYERS, FF, D),
            got["gbias"],
            got["ggain"],
            grad_logits,
        )
        summed = [lax.psum_scatter(part, both, scatter_dimension=1, tiled=True) for part in whole]
        grad_mask = summed[6] * jax.nn.sigmoid(-mask_logits.astype(F32))
        weight_grads, small = tuple(summed[:4]), (summed[4], summed[5], grad_mask)
    return (
        got["out"].reshape(tokens.shape),
        got["gtok"].reshape(tokens.shape),
        *weight_grads,
        *small,
    )


def solution(mesh):
    placed = (
        P("wa", "blk", None, None),
        P("wa", None),
        P(),
        P(None, ("blk", "wa"), None),
        P(None, ("blk", "wa"), None),
        P(None, ("blk", "wa"), None),
        P(None, ("blk", "wa"), None),
        P(None, ("blk", "wa")),
        P(None, ("blk", "wa")),
        P(None, ("blk", "wa")),
        P("wa", "blk", None),
        P("wa", "blk"),
        P("wa", "blk", None, None),
    )
    return jax.shard_map(
        local,
        mesh=mesh,
        in_specs=placed,
        out_specs=(
            P("wa", "blk", None, None),
            P("wa", "blk", None, None),
            P(None, ("blk", "wa"), None),
            P(None, ("blk", "wa"), None),
            P(None, ("blk", "wa"), None),
            P(None, ("blk", "wa"), None),
            P(None, ("blk", "wa")),
            P(None, ("blk", "wa")),
            P(None, ("blk", "wa")),
        ),
        check_vma=False,
    )
```

time: 1570 us -> 76 us (0.05)
  waiting for transfers between devices: 907 us -> 0 us
  blocking collectives: 420 us -> 0 us
  local copies, waits for them, and re-layouts: 103 us -> 0 us
  Pallas kernels: 0 us -> 74.4 us
  other arithmetic: 60.3 us -> 0 us
  matrix products: 55.7 us -> 0 us
    reduce_scatter x8 -> x0, waiting for transfers between devices: 709 us -> none  [the longest x2 265 us: local(): lax.psum_scatter(grad_in, ('blk', 'wa'), scatter_dimension=0, tiled=True)]
    all_gather x8 -> x0, blocking collectives: 340 us -> none  [the longest x2 92.1 us: fetch_forward(): lax.all_gather(w_in[layer_index], ('blk', 'wa'), axis=0, tiled=True)]
    unnamed x14 -> x0, waiting for transfers between devices: 197 us -> none
    unnamed x2 -> x0, blocking collectives: 80.2 us -> none
    pallas_call x0 -> x2, Pallas kernels: none -> 74.4 us  [the longest x1 73.5 us: call_kernel(): pl.pallas_call(kernel, out_shape=[hold(shape, F32) for shape in shapes.va...]
    dot_general x40 -> x0, matrix products: 53.3 us -> none  [the longest x7 12.6 us: contract_rows(): lax.dot_general(left, right, (((0,), (0,)), ((), ())), preferred_element_...]
    concatenate x8 -> x0, local copies, waits for them, and re-layouts: 31.3 us -> none  [the longest x6 31.3 us: attention_backward(): jnp.concatenate([d_keys.reshape(blocks, seq_len, model_width), d_values.r...]
    unnamed x298 -> x0, local copies, waits for them, and re-layouts: 23.9 us -> none
  transfers between devices with their start and end apart: 12 -> 0, of which waited for: 10 -> 0; matrix products, arithmetic and copies ran while one was open for 7% -> 0% of each run, Pallas kernels for 0% -> 0%
where the time goes in v1:
time: 76 us; the launch traced here: 75.9 us
  Pallas kernels  74.4 us (98%)
  between operations  1.46 us (2%)
    pallas_call x1, Pallas kernels, call_kernel(): pl.pallas_call(kernel, out_shape=[hold(shape, F32) for shape in shapes.va...  73.5 us

profile of v1, /device:TPU:1, one launch (start us, length us, event | category | flops | bytes accessed | tf_op | source)
XLA Modules:
  0.0 75.9 jit_solution(14721123918037003707)
XLA Ops:
  1.3 73.5 %encoder.1 = (f32[4,64,256]{2,1,0:T(8,128)S(1)}, f32[4,64,256]{2,1,0:T(8,128)S(1)}, f32[2,8,768]{2,1,0:T(8,128)S(1)}, f32[2,8,256]{2,1,0:T(8,128)S(1)}, f32[2,8,...) custom-call(bf16[4,64,256]{2,1,0:T(8,128)(2,1)} %bitcast.5, ...), custom_call_target="tpu_custom_call" | custom-call | tf_op jit(solution)/shard_map/encoder/pallas_call | solution.py:1043
  74.8 0.9 %write_out.1 = (f32[4,64,256]{2,1,0:T(8,128)}, f32[4,64,256]{2,1,0:T(8,128)}, f32[2,8,768]{2,1,0:T(8,128)}, f32[2,8,256]{2,1,0:T(8,128)}, f32[2,8,1024]{2,1,0:T(...) custom-call(f32[4,64,256]{2,1,0:T(8,128)S(1)} %get-tuple-element.27.refs_0_, ...), custom_call_target="tpu_custom_call" | custom-call | tf_op jit(solution)/shard_map/write_out/pallas_call | solution.py:1055

commit v2 on v1

--- a/solution.py
+++ b/solution.py
@@ -16,7 +16,10 @@
 SEQ = 512
 LAYERS = 2
 BLK_DEV = 4
-HALF = 256
+HALF = 512
+CHUNKS = SEQ // HALF
+FWD = 512
+FWD_CHUNKS = SEQ // FWD
 MY_FF = FF // 2
 NEG = -1e30
 EPS = 1e-05
@@ -29,6 +32,14 @@
 PV_ROWS = 24
 SG_BQ, SG_BV, SG_BI, SG_BO, SG_S1, SG_BD, SG_S2, SG_G1, SG_G2, SG_LG = 0, 1, 2, 6, 8, 10, 12, 14, 16, 24
 SG_ROWS = 40
+SLAB = 16
+SLAB_ROWS = (
+    (SG_BQ, SG_BV, SG_BO),
+    (SG_BO + 1, SG_S1, SG_S1 + 1, SG_BI),
+    (SG_BI + 1, SG_BI + 2, SG_BI + 3),
+    (SG_BI + 3, SG_BD, SG_BD + 1, SG_S2, SG_S2 + 1),
+)
+SLAB_GAINS = (SG_G1, SG_G1 + 1, SG_G2, SG_G2 + 1)
 
 
 def nn(left, right):
@@ -84,6 +95,7 @@
         self.send, self.recv, self.anyone = send, recv, anyone
         self.send_used = self.recv_used = 0
         self.pending = {}
+        self.pending_if = []
 
     def recv_sem(self):
         self.recv_used += 1
@@ -94,6 +106,11 @@
         self.pending[self.send_used - 1] = bytes_like
         return self.send_used - 1
 
+    def send_sem_if(self, condition, bytes_like):
+        self.send_used += 1
+        self.pending_if.append((condition, self.send_used - 1, bytes_like))
+        return self.send_used - 1
+
     def push(self, source, target, send_sem, recv_sem, device):
         remote(source, target, self.send.at[send_sem], self.recv.at[recv_sem], device).start()
 
@@ -103,6 +120,11 @@
     def drain(self):
         for send_sem, bytes_like in self.pending.items():
             remote(bytes_like, bytes_like, self.send.at[send_sem], self.recv.at[0], self.anyone).wait_send()
+        for condition, send_sem, bytes_like in self.pending_if:
+
+            @pl.when(condition)
+            def _():
+                remote(bytes_like, bytes_like, self.send.at[send_sem], self.recv.at[0], self.anyone).wait_send()
 
 
 def remote(source, target, send_sem, recv_sem, device):
@@ -141,7 +163,7 @@
     return jnp.sum(value, axis=0, keepdims=True)
 
 
-SEND_SEMS, RECV_SEMS = 34, 70
+SEND_SEMS, RECV_SEMS = 46, 82
 
 
 def scratch_shapes(n_blk, n_wa, gather):
@@ -161,8 +183,8 @@
         SND1=vmem((n_blk, 2, BS, D), BF16),
         RET0=vmem((n_seq, 2, 2, BS, D), BF16),
         RET1=vmem((n_seq, 2, 2, BS, D), BF16),
-        PSEND=vmem((4 * LAYERS, 2, HALF, D), BF16),
-        PRECV=vmem((4 * LAYERS, 2, HALF, D), BF16),
+        PSEND=vmem((4 * LAYERS, SEQ, D), BF16),
+        PRECV=vmem((4 * LAYERS, SEQ, D), BF16),
         X=vmem((SEQ, D), F32),
         XL=vmem((LAYERS, SEQ, D), BF16),
         QKV=vmem((LAYERS, SEQ, 384), BF16),
@@ -194,9 +216,9 @@
         BIAS=vmem((LAYERS, 2, NB, SEQ), F32),
         LR=vmem((2, NB, SEQ), F32),
         SGL=vmem((LAYERS, SG_ROWS, 128), F32),
-        SGF=vmem((2, LAYERS, SG_ROWS, 128), F32),
+        SGF=vmem((2, LAYERS, SLAB if gather else SG_ROWS, 128), F32),
         link_send=pltpu.SemaphoreType.DMA((SEND_SEMS if gather else 8,)),
-        link_recv=pltpu.SemaphoreType.DMA((RECV_SEMS if gather else 12,)),
+        link_recv=pltpu.SemaphoreType.DMA((RECV_SEMS if gather else 16,)),
         tok_send=pltpu.SemaphoreType.DMA((3,)),
         tok_recv=pltpu.SemaphoreType.DMA((3,)),
         ret_send=pltpu.SemaphoreType.DMA((2,)),
@@ -217,10 +239,11 @@
             SP=vmem((n_blk, n_plane, 2, 8, 128), F32),
             FX=vmem((LAYERS, 8, 1024), F32),
             RX=vmem((LAYERS, 8, 1024), F32),
-            SGP=vmem((LAYERS, n_plane - 1, SG_ROWS, 128), F32),
-            SGS=vmem((LAYERS, SG_ROWS, 128), F32),
-            SGZ=vmem((LAYERS, n_blk - 1, SG_ROWS, 128), F32),
-            BT=vmem((LAYERS, PV_ROWS, 128), F32),
+            SLO=vmem((LAYERS, n_blk, SLAB, 128), BF16),
+            SLP=vmem((LAYERS, n_plane - 1, n_blk, SLAB, 128), BF16),
+            SLS=vmem((LAYERS, n_blk, SLAB, 128), BF16),
+            SLZ=vmem((LAYERS, n_blk - 1, SLAB, 128), BF16),
+            BT=vmem((LAYERS, 8, 128), F32),
         )
         for kind, (rows, cols) in RS_KINDS.items():
             shapes["G_" + kind] = vmem((LAYERS, n_blk, n_plane, rows, cols), BF16)
@@ -230,6 +253,7 @@
     return shapes
 
 
+RS_STRAIGHT = {("q", 0)}
 RS_KINDS = {"d": (32, D), "i": (16, MY_FF), "o": (16, 128), "q": (16, 384)}
 
 
@@ -250,6 +274,9 @@
         partner = (z, p * 2 + (1 - c))
         links = Links(r["link_send"], r["link_recv"], partner)
         x_peer, y_peer = (z, w ^ 2), (z, w ^ 4)
+        in_middle = jnp.logical_or(z == 1, z == 2)
+        z_next, z_far = (z ^ 1, w), (2 - lax.div(z, 2), w)
+        far_pair = pl.ds(2 - 2 * lax.div(z, 2), 2)
         local_sems = r["local_sems"]
         my_cols = pl.ds(pl.multiple_of(c * 128, 128), 128)
         other_cols = pl.ds(pl.multiple_of((1 - c) * 128, 128), 128)
@@ -374,9 +401,11 @@
             ag_send = {}
             for kind in (0, 1, 2):
                 ref = weight_refs[kind]
-                likes = (ref.at[:, 0, 0:3], ref.at[0], ref.at[0, 0:2])
+                likes = (ref.at[:, 0:2, 0], ref.at[0], ref.at[0, 0:2])
                 ag_send[kind] = [links.send_sem(like) for like in likes]
-            ag_send["small"] = [links.send_sem(like) for like in (SP.at[0, 0:3], SP.at[:, 0:2], SP.at[0:2, 0:2])]
+                ag_send[kind].append(links.send_sem_if(in_middle, likes[0]))
+            ag_send["small"] = [links.send_sem(like) for like in (SP.at[0:2, 0], SP.at[:, 0:2], SP.at[0:2, 0:2])]
+            ag_send["small"].append(links.send_sem_if(in_middle, SP.at[0:2, 0]))
 
             def rows_at(name, z_at, p_at):
                 if name == "small":
@@ -386,17 +415,22 @@
             def ag_push(name, stage, z_at, p_at, device):
                 ref = rows_at(name, z_at, p_at)
                 send_sem = ag_send[name if name == "small" else name[0]][stage]
-                links.push(ref, ref, send_sem, ag_recv[name][stage], device)
+                links.push(ref, ref, send_sem, ag_recv[name][stage % 3], device)
 
             every, z_low, z_high = slice(0, 4), slice(0, 2), slice(2, 4)
 
             def ag_z(name):
                 ag_recv[name] = [links.recv_sem() for _ in range(3)]
-                for m in range(1, n_blk):
-                    ag_push(name, 0, z, p, (z ^ m, w))
+                ag_push(name, 0, z, p, z_far)
+                ag_push(name, 0, z, p, z_next)
 
             def ag_xy(name):
                 links.arrived(rows_at(name, 0, slice(0, 3)), ag_recv[name][0])
+
+                @pl.when(in_middle)
+                def _():
+                    ag_push(name, 3, far_pair, p, z_next)
+
                 ag_push(name, 1, every, p, x_peer)
                 ag_push(name, 1, every, p, y_peer)
 
@@ -427,23 +461,21 @@
         if gather:
             merge_rows(0, 1)
             merge_rows(1, 1)
+            ag_z((0, 1))
+            ag_z((1, 1))
+            ag_z((2, 1))
             ag_xy((0, 0))
             ag_xy("small")
             ag_xy((1, 0))
             ag_xy((2, 0))
-            ag_z((0, 1))
             ag_pass((0, 0))
             ag_pass("small")
-            ag_z((1, 1))
-            ag_z((2, 1))
             ag_pass((1, 0))
             ag_pass((2, 0))
 
         take_kind(0)
         tokens_in = links.recv_sem()
         links.push(TOK.at[:, c], TOK.at[:, c], links.send_sem(TOK.at[:, 0]), tokens_in, partner)
-        if gather:
-            ag_xy((0, 1))
         links.arrived(PGV.at[0], place_in)
         to_scalars = pltpu.make_async_copy(PGV, PGS, local_sems.at[3])
         to_scalars.start()
@@ -508,19 +540,28 @@
 
         PSEND, PRECV = r["PSEND"], r["PRECV"]
         exchange_out = links.send_sem(PSEND)
-        exchange_in = [links.recv_sem() for _ in range(4)]
+        most = max(CHUNKS, FWD_CHUNKS)
+        exchange_in = [links.recv_sem() for _ in range(2 * most)]
+
+        def part_of(step, chunk):
+            size = FWD if step < 2 * LAYERS else HALF
+            return pl.ds(chunk * size, size)
 
         def give(step, chunk, value):
-            PSEND[step, chunk] = value.astype(BF16)
-            sem = exchange_in[2 * (step % 2) + chunk]
-            links.push(PSEND.at[step, chunk], PRECV.at[step, chunk], exchange_out, sem, partner)
+            part = part_of(step, chunk)
+            PSEND[step, part] = value.astype(BF16)
+            sem = exchange_in[most * (step % 2) + chunk]
+            links.push(PSEND.at[step, part], PRECV.at[step, part], exchange_out, sem, partner)
 
         def take(step, chunk):
-            links.arrived(PRECV.at[step, chunk], exchange_in[2 * (step % 2) + chunk])
+            links.arrived(PRECV.at[step, part_of(step, chunk)], exchange_in[most * (step % 2) + chunk])
 
         def of_head(value, h):
             keep = (lanes(value.shape) // HD) == h
             return jnp.where(keep, value, jnp.zeros_like(value))
+
+        def fwd_rows(chunk):
+            return slice(chunk * FWD, (chunk + 1) * FWD)
 
         def rows_of(chunk):
             return slice(chunk * HALF, (chunk + 1) * HALF)
@@ -576,71 +617,74 @@
                 WO[l, :, my_cols] = WA[l, pl.ds(c * part, part), :, :, 384:512].reshape(128, 128)
             bias = jnp.concatenate([mine(l, ROW_BQ), jnp.zeros((1, 128), F32), mine(l, ROW_BV)], axis=1)
             scale = jnp.where(lanes((1, 384)) < 128, 0.125, 1.0)
-            for chunk in range(2):
-                rows = rows_of(chunk)
+            for chunk in range(FWD_CHUNKS):
+                rows = fwd_rows(chunk)
                 QKV[l, rows] = ((nn(XL[l, rows], weight_qkv(l)) + bias) * scale).astype(BF16)
             keys = QKV[l, :, 128:256]
-            KT[l] = keys.astype(F32).T.astype(BF16)
             VT[...] = QKV[l, :, 256:384].astype(F32).T.astype(BF16)
             if gather:
                 if l + 1 < LAYERS:
-                    ag_xy((1, l + 1))
-                    ag_xy((2, l + 1))
+                    ag_xy((0, l + 1))
                 links.arrived(r["WOX"].at[l], wo_in)
                 WO[l, :, other_cols] = r["WOX"][l].reshape(128, 128)
-            for chunk in range(2):
-                rows = rows_of(chunk)
+            for chunk in range(FWD_CHUNKS):
+                rows = fwd_rows(chunk)
                 for h in (0, 1):
                     queries = of_head(QKV[l, rows, 0:128], h)
-                    ST[...] = nt(keys, queries)
-                    top = jnp.full((8, HALF), NEG, F32)
+                    ST[:, 0:FWD] = nt(keys, queries)
+                    top = jnp.full((8, FWD), NEG, F32)
                     for kb in range(NB):
-                        score = ST[kb * BS : (kb + 1) * BS] + BIAS[l, h, kb : kb + 1, rows]
-                        top = jnp.maximum(top, jnp.max(score.reshape(8, 8, HALF), axis=0))
+                        score = ST[kb * BS : (kb + 1) * BS, 0:FWD] + BIAS[l, h, kb : kb + 1, rows]
+                        top = jnp.maximum(top, jnp.max(score.reshape(8, 8, FWD), axis=0))
                     top = jnp.max(top, axis=0, keepdims=True)
-                    total = jnp.zeros((8, HALF), F32)
+                    total = jnp.zeros((8, FWD), F32)
                     for kb in range(NB):
-                        score = ST[kb * BS : (kb + 1) * BS] + BIAS[l, h, kb : kb + 1, rows]
+                        score = ST[kb * BS : (kb + 1) * BS, 0:FWD] + BIAS[l, h, kb : kb + 1, rows]
                         weight_of = jnp.exp(score - top)
-                        ST[kb * BS : (kb + 1) * BS] = weight_of
+                        ST[kb * BS : (kb + 1) * BS, 0:FWD] = weight_of
                         total = total + fold(weight_of)
                     inverse = 1.0 / column_sum(total)
                     for kb in range(NB):
-                        PR[l, h, kb * BS : (kb + 1) * BS, rows] = (ST[kb * BS : (kb + 1) * BS] * inverse).astype(BF16)
+                        PR[l, h, kb * BS : (kb + 1) * BS, rows] = (ST[kb * BS : (kb + 1) * BS, 0:FWD] * inverse).astype(BF16)
                     AT[l, h * HD : (h + 1) * HD, rows] = nn(VT[h * HD : (h + 1) * HD], PR[l, h, :, rows])
                 AN[l, rows] = AT[l, :, rows].T.astype(BF16)
                 branch = nn(AN[l, rows], WO[l])
                 give(step, chunk, branch)
                 PO[rows] = X[rows] + branch + wide(l, ROW_BO)
-                part = pl.ds(chunk * HALF, HALF)
+                part = pl.ds(chunk * FWD, FWD)
                 links.push(AN.at[l, part], AX.at[l, part], attended_out, attended_in, partner)
+            KT[l] = keys.astype(F32).T.astype(BF16)
+            if l == LAYERS - 1:
+                take_kind(1)
+                take_kind(2)
+                grads_in = links.recv_sem()
+                links.push(MG.at[:, c], MG.at[:, c], links.send_sem(MG.at[:, 0]), grads_in, partner)
             if gather:
                 if l + 1 < LAYERS:
-                    ag_pass((0, l + 1))
-                    ag_pass((1, l + 1))
-                    ag_pass((2, l + 1))
+                    ag_xy((1, l + 1))
+                    ag_xy((2, l + 1))
                 ag_ready((1, l))
                 ag_ready((2, l))
-            for chunk in range(2):
-                rows = rows_of(chunk)
+            for chunk in range(FWD_CHUNKS):
+                rows = fwd_rows(chunk)
                 take(step, chunk)
                 gain, shift = wide(l, ROW_G1), wide(l, ROW_S1)
-                for t in range(0, HALF, BS):
-                    tile = slice(chunk * HALF + t, chunk * HALF + t + BS)
-                    hidden = PO[tile] + PRECV[step, chunk, t : t + BS].astype(F32)
+                for t in range(0, FWD, BS):
+                    tile = slice(chunk * FWD + t, chunk * FWD + t + BS)
+                    hidden = PO[tile] + PRECV[step, tile].astype(F32)
                     normed, unit, rstd = layer_norm(hidden, gain, shift)
                     U1[l, tile] = unit
                     R1[l, tile] = rstd
                     X[tile] = normed
                     Y1B[l, tile] = normed.astype(BF16)
-                FS[...] = nn(Y1B[l, rows], weight(1, l))
+                FS[0:FWD] = nn(Y1B[l, rows], weight(1, l))
                 inner_bias = []
                 for t in range(4):
                     row = ROW_BI + 2 * t
                     inner_bias.append(pick_groups(PV[l, row : row + 1, :], PV[l, row + 1 : row + 2, :], c))
                 inner_bias = jnp.concatenate(inner_bias, axis=1)
-                for t in range(0, HALF, 32):
-                    tile = slice(chunk * HALF + t, chunk * HALF + t + 32)
+                for t in range(0, FWD, 32):
+                    tile = slice(chunk * FWD + t, chunk * FWD + t + 32)
                     inner = FS[t : t + 32] + inner_bias
                     below = 0.5 + 0.5 * lax.erf(inner * 0.7071067811865476)
                     G[l, tile] = (inner * below).astype(BF16)
@@ -649,12 +693,17 @@
                 branch = nn(G[l, rows], weight(2, l))
                 give(step + 1, chunk, branch)
                 PO[rows] = X[rows] + branch + wide(l, ROW_BD)
-            for chunk in range(2):
+                if gather and l + 1 < LAYERS and chunk == 0:
+                    ag_pass((0, l + 1))
+            if gather and l + 1 < LAYERS:
+                ag_pass((1, l + 1))
+                ag_pass((2, l + 1))
+            for chunk in range(FWD_CHUNKS):
                 take(step + 1, chunk)
                 gain, shift = wide(l, ROW_G2), wide(l, ROW_S2)
-                for t in range(0, HALF, BS):
-                    tile = slice(chunk * HALF + t, chunk * HALF + t + BS)
-                    hidden = PO[tile] + PRECV[step + 1, chunk, t : t + BS].astype(F32)
+                for t in range(0, FWD, BS):
+                    tile = slice(chunk * FWD + t, chunk * FWD + t + BS)
+                    hidden = PO[tile] + PRECV[step + 1, tile].astype(F32)
                     normed, unit, rstd = layer_norm(hidden, gain, shift)
                     U2[l, tile] = unit
                     R2[l, tile] = rstd
@@ -662,15 +711,11 @@
                     if l + 1 < LAYERS:
                         XL[l + 1, tile] = normed.astype(BF16)
                     else:
-                        YB[0][chunk * 4 + t // BS] = normed.astype(BF16)
+                        YB[0][(chunk * FWD + t) // BS] = normed.astype(BF16)
         send_back(0)
 
         DY, DD, DF, DH, DO, DA, DAT, DQKV = (r[n] for n in ("DY", "DD", "DF", "DH", "DO", "DA", "DAT", "DQKV"))
         LR, SGL = r["LR"], r["SGL"]
-        take_kind(1)
-        take_kind(2)
-        grads_in = links.recv_sem()
-        links.push(MG.at[:, c], MG.at[:, c], links.send_sem(MG.at[:, 0]), grads_in, partner)
         links.arrived(MG.at[:, 0], grads_in)
         wanted = []
         lane = lanes((1, 128))
@@ -678,7 +723,7 @@
             wanted.append(jnp.where(lane < 64, MR[2 * t, 0:1, :], MR[2 * t + 1, 0:1, :]))
         wanted = jnp.concatenate(wanted, axis=1) - seq * SEQ
         listed = MG[...].reshape(n_blk * 64, D)
-        for chunk in range(2):
+        for chunk in range(CHUNKS):
             row_ids = lax.broadcasted_iota(jnp.int32, (HALF, n_blk * 64), 0) + chunk * HALF
             DY[rows_of(chunk)] = nn((row_ids == wanted).astype(F32).astype(BF16), listed)
 
@@ -692,13 +737,19 @@
             rs_recv[kind, l] = [links.recv_sem() for _ in range(3)]
             grad, parts, sem = r["G_" + kind], r["RP_" + kind], rs_recv[kind, l][0]
             out = rs_out[kind][0]
+            if (kind, l) in RS_STRAIGHT:
+                devices = (x_peer, y_peer, (z, w ^ 6))
+                for m in range(3):
+                    links.push(grad.at[l, z_low, p ^ (m + 1)], parts.at[l, 0, m], out, sem, devices[m])
+                    links.push(grad.at[l, z_high, p ^ (m + 1)], parts.at[l, 1, m], out, sem, devices[m])
+                return
             links.push(grad.at[l, z_low, p ^ 3], parts.at[l, 0, 1], out, sem, x_peer)
             links.push(grad.at[l, z_high, p ^ 3], parts.at[l, 1, 1], out, sem, y_peer)
             links.push(grad.at[l, z_low, p ^ 1], parts.at[l, 0, 0], out, sem, x_peer)
             links.push(grad.at[l, z_high, p ^ 2], parts.at[l, 1, 0], out, sem, y_peer)
 
         def rs_pass(kind, l):
-            if not gather:
+            if not gather or (kind, l) in RS_STRAIGHT:
                 return
             grad, parts, sem = r["G_" + kind], r["RP_" + kind], rs_recv[kind, l][1]
             links.arrived(parts.at[l, :, 0:2], rs_recv[kind, l][0])
@@ -711,9 +762,17 @@
             if not gather:
                 return
             grad, parts, total = r["G_" + kind], r["RP_" + kind], r["SZ_" + kind]
-            links.arrived(parts.at[l, :, 2], rs_recv[kind, l][1])
-            for half, straight, passed in ((z_low, 0, 1), (z_high, 1, 0)):
-                value = grad[l, half, p].astype(F32) + parts[l, straight, 0].astype(F32) + parts[l, passed, 2].astype(F32)
+            if (kind, l) in RS_STRAIGHT:
+                links.arrived(parts.at[l], rs_recv[kind, l][0])
+            else:
+                links.arrived(parts.at[l, :, 2], rs_recv[kind, l][1])
+            for at, half in enumerate((z_low, z_high)):
+                value = grad[l, half, p].astype(F32)
+                if (kind, l) in RS_STRAIGHT:
+                    for m in range(3):
+                        value = value + parts[l, at, m].astype(F32)
+                else:
+                    value = value + parts[l, at, 0].astype(F32) + parts[l, 1 - at, 2].astype(F32)
                 total[l, half] = value.astype(BF16)
             for m in range(1, n_blk):
                 links.push(total.at[l, z ^ m], r["RZ_" + kind].at[l, m - 1], rs_out[kind][1], rs_recv[kind, l][2], (z ^ m, w))
@@ -727,31 +786,39 @@
 
         sg_recv = {}
         if gather:
-            sg_out = (links.send_sem(r["SGP"]), links.send_sem(r["SGZ"]))
+            SLO, SLP, SLS, SLZ = (r[name] for name in ("SLO", "SLP", "SLS", "SLZ"))
+            sg_out = (links.send_sem(SLP), links.send_sem(SLZ))
 
         def small_start(l):
             if not gather:
                 return
+            for owner in range(n_blk):
+                parts = [SGL[l, at : at + 1, :] for at in SLAB_ROWS[owner]]
+                parts += [jnp.zeros((1, 128), F32)] * (5 - len(parts))
+                parts += [SGL[l, SLAB_GAINS[owner] : SLAB_GAINS[owner] + 1, :], jnp.zeros((2, 128), F32)]
+                at = SG_LG + 8 * (owner % 2)
+                slab = jnp.concatenate(parts + [SGL[l, at : at + 8, :]], axis=0)
+                SLO[l, owner] = slab.astype(BF16)
             sg_recv[l] = [links.recv_sem() for _ in range(2)]
             for m in range(1, n_plane):
-                links.push(SGL.at[l], r["SGP"].at[l, m - 1], sg_out[0], sg_recv[l][0], (z, w ^ (2 * m)))
+                links.push(SLO.at[l], SLP.at[l, m - 1], sg_out[0], sg_recv[l][0], (z, w ^ (2 * m)))
 
         def small_z(l):
             if not gather:
                 return
-            links.arrived(r["SGP"].at[l], sg_recv[l][0])
-            total = SGL[l]
+            links.arrived(SLP.at[l], sg_recv[l][0])
+            total = SLO[l].astype(F32)
             for m in range(1, n_plane):
-                total = total + r["SGP"][l, m - 1]
-            r["SGS"][l] = total
+                total = total + SLP[l, m - 1].astype(F32)
+            SLS[l] = total.astype(BF16)
             for m in range(1, n_blk):
-                links.push(r["SGS"].at[l], r["SGZ"].at[l, m - 1], sg_out[1], sg_recv[l][1], (z ^ m, w))
+                links.push(SLS.at[l, z ^ m], SLZ.at[l, m - 1], sg_out[1], sg_recv[l][1], (z ^ m, w))
 
         def small_end(l):
-            links.arrived(r["SGZ"].at[l], sg_recv[l][1])
-            total = r["SGS"][l]
+            links.arrived(SLZ.at[l], sg_recv[l][1])
+            total = SLS[l, z].astype(F32)
             for m in range(1, n_blk):
-                total = total + r["SGZ"][l, m - 1]
+                total = total + SLZ[l, m - 1].astype(F32)
             return total
 
         def store_grad(kind, l, value):
@@ -771,7 +838,7 @@
             gain = wide(l, ROW_G2)
             sums = [jnp.zeros((8, D), F32) for _ in range(3)]
             inner_sum = jnp.zeros((8, MY_FF), F32)
-            for chunk in range(2):
+            for chunk in range(CHUNKS):
                 rows = rows_of(chunk)
                 for t in range(0, HALF, BS):
                     tile = slice(chunk * HALF + t, chunk * HALF + t + BS)
@@ -779,7 +846,7 @@
                     if l < LAYERS - 1:
                         if t == 0:
                             take(step - 1, chunk)
-                        grad = grad + PRECV[step - 1, chunk, t : t + BS].astype(F32)
+                        grad = grad + PRECV[step - 1, tile].astype(F32)
                     d_hidden = layer_norm_back(grad, unit, R2[l, tile], gain)
                     low = d_hidden.astype(BF16)
                     DH[tile] = d_hidden
@@ -811,12 +878,12 @@
                 rs_z("d", l + 1)
             gain = wide(l, ROW_G1)
             sums = [jnp.zeros((8, D), F32) for _ in range(3)]
-            for chunk in range(2):
+            for chunk in range(CHUNKS):
                 rows = rows_of(chunk)
                 take(step, chunk)
                 for t in range(0, HALF, BS):
                     tile = slice(chunk * HALF + t, chunk * HALF + t + BS)
-                    grad = DH[tile] + PRECV[step, chunk, t : t + BS].astype(F32)
+                    grad = DH[tile] + PRECV[step, tile].astype(F32)
                     unit = U1[l, tile]
                     d_hidden = layer_norm_back(grad, unit, R1[l, tile], gain)
                     low = d_hidden.astype(BF16)
@@ -847,7 +914,7 @@
                 rs_z("i", l + 1)
                 small_z(l + 1)
             keys, values = QKV[l, :, 128:256], QKV[l, :, 256:384]
-            for chunk in range(2):
+            for chunk in range(CHUNKS):
                 rows = rows_of(chunk)
                 d_query = []
                 for h in (0, 1):
@@ -863,11 +930,16 @@
                 d_query = jnp.concatenate(d_query, axis=0) * 0.125
                 DQKV[rows, 0:128] = d_query.T.astype(BF16)
                 if l == LAYERS - 1:
-                    if chunk == 1:
+                    if chunk == CHUNKS - 1:
                         rs_pass("d", l)
-                else:
-                    rs_z("oq"[chunk], l + 1)
-                    rs_pass("di"[chunk], l)
+                elif chunk == -1:
+                    rs_z("o", l + 1)
+                    rs_pass("d", l)
+                elif chunk == CHUNKS - 1:
+                    rs_z("o", l + 1)
+                    rs_pass("d", l)
+                    rs_z("q", l + 1)
+                    rs_pass("i", l)
             d_keys = jnp.zeros((SEQ, 128), F32)
             d_values = jnp.zeros((SEQ, 128), F32)
             for h in (0, 1):
@@ -882,7 +954,7 @@
                     LR[h], by_block, (((1,), (1,)), ((), ())), preferred_element_type=F32, precision=HIGHEST
                 )
                 SGL[l, SG_LG + 8 * h : SG_LG + 8 * h + 8, :] = table
-            for chunk in range(2):
+            for chunk in range(CHUNKS):
                 rows = rows_of(chunk)
                 branch = nt(DQKV[rows], weight_qkv(l))
                 give(step + 1, chunk, branch)
@@ -895,17 +967,17 @@
             if l == LAYERS - 1:
                 rs_pass("i", l)
             rs_pass("o", l)
-        for chunk in range(2):
+        for chunk in range(CHUNKS):
             take(step + 1, chunk)
             for t in range(0, HALF, BS):
                 tile = slice(chunk * HALF + t, chunk * HALF + t + BS)
-                grad = DY[tile] + PRECV[step + 1, chunk, t : t + BS].astype(F32)
-                YB[1][chunk * 4 + t // BS] = grad.astype(BF16)
+                grad = DY[tile] + PRECV[step + 1, tile].astype(F32)
+                YB[1][(chunk * HALF + t) // BS] = grad.astype(BF16)
+        rs_z("d", 0)
+        rs_z("i", 0)
         send_back(1)
         SGF = r["SGF"]
         if gather:
-            rs_z("d", 0)
-            rs_z("i", 0)
             rs_pass("q", 0)
             rs_z("o", 0)
             small_z(0)
@@ -942,24 +1014,52 @@
             SGF[1 - c] = jnp.zeros(SGL.shape, F32)
         for l in range(LAYERS):
 
+            def row(core, at):
+                return SGF[core, l, at : at + 1, :]
+
+            if gather:
+                woven = [weave_groups(row(0, at), row(1, at)) for at in (0, 1, 2, 3)]
+                tiles = (
+                    (row(0, 0), row(1, 0), row(0, 1), row(1, 1), row(0, 2)),
+                    (row(0, 0), row(0, 1), row(0, 2), *woven[3]),
+                    (*woven[0], *woven[1], woven[2][0]),
+                    (woven[0][1], row(0, 1), row(0, 2), row(0, 3), row(0, 4)),
+                )
+                for t in range(5):
+                    choice = tiles[0][t]
+                    for owner in range(1, n_blk):
+                        choice = jnp.where(z == owner, tiles[owner][t], choice)
+                    r["BT"][l, t : t + 1, :] = choice
+                lane = lanes((1, 128))
+                start = w * widths[0]
+                tile, offset = lax.div(start, 128), lax.rem(start, 128)
+                shift = lax.rem(128 - offset, 128)
+                first = pltpu.roll(r["BT"][l, pl.ds(tile, 1), :], shift, 1)
+                second = pltpu.roll(r["BT"][l, pl.ds(tile + 1, 1), :], shift, 1)
+                r["gbias"][l : l + 1, :] = jnp.where(lane < 128 - offset, first, second)[:, 0 : widths[0]]
+                gain = pltpu.roll(row(0, 5), lax.rem(128 - w * widths[1], 128), 1)
+                r["ggain"][l : l + 1, :] = gain[:, 0 : widths[1]]
+                table = SGF[lax.div(z, 2), l, 8:16, :]
+                wide_lane = lanes((8, 128))
+                column = jnp.sum(jnp.where(wide_lane == w, table, 0.0), axis=1, keepdims=True)
+                diagonal = wide_lane == lax.broadcasted_iota(jnp.int32, (8, 128), 0)
+                values_row = column_sum(jnp.where(diagonal, column, 0.0))[:, 0:NB]
+                logit = r["mask_logits"][...].astype(F32)[l : l + 1]
+                r["glog"][l : l + 1, :] = values_row / (1.0 + jnp.exp(logit))
+                continue
+
             def put(at, value):
-                if gather:
-                    r["BT"][l, at : at + 1, :] = value
-                elif at < ROW_G1:
+                if at < ROW_G1:
                     r["gbias"][l : l + 1, 128 * at : 128 * at + 128] = value
                 else:
                     at -= ROW_G1
                     r["ggain"][l : l + 1, 128 * at : 128 * at + 128] = value
 
-            def row(core, at):
-                return SGF[core, l, at : at + 1, :]
-
             for core in (0, 1):
                 put(ROW_BQ + core, row(core, SG_BQ))
                 put(ROW_BV + core, row(core, SG_BV))
-                if not gather:
-                    for h in (0, 1):
-                        r["glog"][l, 2 * core + h] = SGF[core, l, SG_LG + 8 * h : SG_LG + 8 * h + 8, :]
+                for h in (0, 1):
+                    r["glog"][l, 2 * core + h] = SGF[core, l, SG_LG + 8 * h : SG_LG + 8 * h + 8, :]
             singles = ((ROW_BO, SG_BO), (ROW_S1, SG_S1), (ROW_BD, SG_BD), (ROW_S2, SG_S2), (ROW_G1, SG_G1), (ROW_G2, SG_G2))
             for at, source in singles:
                 for j in (0, 1):
@@ -968,29 +1068,6 @@
                 first, second = weave_groups(row(0, SG_BI + t), row(1, SG_BI + t))
                 put(ROW_BI + 2 * t, first)
                 put(ROW_BI + 2 * t + 1, second)
-            if gather:
-                index = z * n_wa + w
-                lane = lanes((1, 128))
-
-                def entries(first_row, width):
-                    start = index * width
-                    tile, offset = lax.div(start, 128), lax.rem(start, 128)
-                    shift = lax.rem(128 - offset, 128)
-                    first = pltpu.roll(r["BT"][l, pl.ds(first_row + tile, 1), :], shift, 1)
-                    if 128 % width == 0:
-                        return first[:, 0:width]
-                    second = pltpu.roll(r["BT"][l, pl.ds(first_row + tile + 1, 1), :], shift, 1)
-                    return jnp.where(lane < 128 - offset, first, second)[:, 0:width]
-
-                r["gbias"][l : l + 1, :] = entries(0, widths[0])
-                r["ggain"][l : l + 1, :] = entries(ROW_G1, widths[1])
-                table = SGF[lax.div(z, 2), l, pl.ds(SG_LG + 8 * lax.rem(z, 2), 8), :]
-                wide_lane = lanes((8, 128))
-                column = jnp.sum(jnp.where(wide_lane == w, table, 0.0), axis=1, keepdims=True)
-                diagonal = wide_lane == lax.broadcasted_iota(jnp.int32, (8, 128), 0)
-                values_row = column_sum(jnp.where(diagonal, column, 0.0))[:, 0:NB]
-                logit = r["mask_logits"][...].astype(F32)[l : l + 1]
-                r["glog"][l : l + 1, :] = values_row / (1.0 + jnp.exp(logit))
         if gather:
             links.arrived(RX, fx_in)
             for l in range(LAYERS):

time: 76 us -> 71 us (0.934)
  Pallas kernels: 74.4 us -> 69.4 us
    pallas_call x1, Pallas kernels: 73.5 us -> 68.4 us  [call_kernel(): pl.pallas_call(kernel, out_shape=[hold(shape, F32) for shape in shapes.va...]
where the time goes in v2:
time: 71 us; the launch traced here: 70.8 us
  Pallas kernels  69.4 us (98%)
  between operations  1.46 us (2%)
    pallas_call x1, Pallas kernels, call_kernel(): pl.pallas_call(kernel, out_shape=[hold(shape, F32) for shape in shapes.va...  68.4 us

profile of v2, /device:TPU:1, one launch (start us, length us, event | category | flops | bytes accessed | tf_op | source)
XLA Modules:
  0.0 70.8 jit_solution(13092678073582015013)
XLA Ops:
  1.3 68.4 %encoder.1 = (f32[4,64,256]{2,1,0:T(8,128)S(1)}, f32[4,64,256]{2,1,0:T(8,128)S(1)}, f32[2,8,768]{2,1,0:T(8,128)S(1)}, f32[2,8,256]{2,1,0:T(8,128)S(1)}, f32[2,8,...) custom-call(bf16[4,64,256]{2,1,0:T(8,128)(2,1)} %bitcast.5, ...), custom_call_target="tpu_custom_call" | custom-call | tf_op jit(solution)/shard_map/encoder/pallas_call | solution.py:1120
  69.7 0.9 %write_out.1 = (f32[4,64,256]{2,1,0:T(8,128)}, f32[4,64,256]{2,1,0:T(8,128)}, f32[2,8,768]{2,1,0:T(8,128)}, f32[2,8,256]{2,1,0:T(8,128)}, f32[2,8,1024]{2,1,0:T(...) custom-call(f32[4,64,256]{2,1,0:T(8,128)S(1)} %get-tuple-element.27.refs_0_, ...), custom_call_target="tpu_custom_call" | custom-call | tf_op jit(solution)/shard_map/write_out/pallas_call | solution.py:1132

commit v3 on v2

--- a/solution.py
+++ b/solution.py
@@ -253,7 +253,6 @@
     return shapes
 
 
-RS_STRAIGHT = {("q", 0)}
 RS_KINDS = {"d": (32, D), "i": (16, MY_FF), "o": (16, 128), "q": (16, 384)}
 
 
@@ -625,6 +624,8 @@
             if gather:
                 if l + 1 < LAYERS:
                     ag_xy((0, l + 1))
+                    ag_xy((1, l + 1))
+                    ag_xy((2, l + 1))
                 links.arrived(r["WOX"].at[l], wo_in)
                 WO[l, :, other_cols] = r["WOX"][l].reshape(128, 128)
             for chunk in range(FWD_CHUNKS):
@@ -661,8 +662,7 @@
                 links.push(MG.at[:, c], MG.at[:, c], links.send_sem(MG.at[:, 0]), grads_in, partner)
             if gather:
                 if l + 1 < LAYERS:
-                    ag_xy((1, l + 1))
-                    ag_xy((2, l + 1))
+                    ag_pass((0, l + 1))
                 ag_ready((1, l))
                 ag_ready((2, l))
             for chunk in range(FWD_CHUNKS):
@@ -693,8 +693,6 @@
                 branch = nn(G[l, rows], weight(2, l))
                 give(step + 1, chunk, branch)
                 PO[rows] = X[rows] + branch + wide(l, ROW_BD)
-                if gather and l + 1 < LAYERS and chunk == 0:
-                    ag_pass((0, l + 1))
             if gather and l + 1 < LAYERS:
                 ag_pass((1, l + 1))
                 ag_pass((2, l + 1))
@@ -734,52 +732,30 @@
         def rs_start(kind, l):
             if not gather:
                 return
-            rs_recv[kind, l] = [links.recv_sem() for _ in range(3)]
+            rs_recv[kind, l] = [links.recv_sem() for _ in range(2)]
             grad, parts, sem = r["G_" + kind], r["RP_" + kind], rs_recv[kind, l][0]
             out = rs_out[kind][0]
-            if (kind, l) in RS_STRAIGHT:
-                devices = (x_peer, y_peer, (z, w ^ 6))
-                for m in range(3):
-                    links.push(grad.at[l, z_low, p ^ (m + 1)], parts.at[l, 0, m], out, sem, devices[m])
-                    links.push(grad.at[l, z_high, p ^ (m + 1)], parts.at[l, 1, m], out, sem, devices[m])
-                return
-            links.push(grad.at[l, z_low, p ^ 3], parts.at[l, 0, 1], out, sem, x_peer)
-            links.push(grad.at[l, z_high, p ^ 3], parts.at[l, 1, 1], out, sem, y_peer)
-            links.push(grad.at[l, z_low, p ^ 1], parts.at[l, 0, 0], out, sem, x_peer)
-            links.push(grad.at[l, z_high, p ^ 2], parts.at[l, 1, 0], out, sem, y_peer)
-
-        def rs_pass(kind, l):
-            if not gather or (kind, l) in RS_STRAIGHT:
-                return
-            grad, parts, sem = r["G_" + kind], r["RP_" + kind], rs_recv[kind, l][1]
-            links.arrived(parts.at[l, :, 0:2], rs_recv[kind, l][0])
-            parts[l, 0, 1] = (grad[l, z_low, p ^ 2].astype(F32) + parts[l, 0, 1].astype(F32)).astype(BF16)
-            links.push(parts.at[l, 0, 1], parts.at[l, 1, 2], rs_out[kind][0], sem, y_peer)
-            parts[l, 1, 1] = (grad[l, z_high, p ^ 1].astype(F32) + parts[l, 1, 1].astype(F32)).astype(BF16)
-            links.push(parts.at[l, 1, 1], parts.at[l, 0, 2], rs_out[kind][0], sem, x_peer)
+            devices = (x_peer, y_peer, (z, w ^ 6))
+            for m in range(3):
+                links.push(grad.at[l, z_low, p ^ (m + 1)], parts.at[l, 0, m], out, sem, devices[m])
+                links.push(grad.at[l, z_high, p ^ (m + 1)], parts.at[l, 1, m], out, sem, devices[m])
 
         def rs_z(kind, l):
             if not gather:
                 return
             grad, parts, total = r["G_" + kind], r["RP_" + kind], r["SZ_" + kind]
-            if (kind, l) in RS_STRAIGHT:
-                links.arrived(parts.at[l], rs_recv[kind, l][0])
-            else:
-                links.arrived(parts.at[l, :, 2], rs_recv[kind, l][1])
+            links.arrived(parts.at[l], rs_recv[kind, l][0])
             for at, half in enumerate((z_low, z_high)):
                 value = grad[l, half, p].astype(F32)
-                if (kind, l) in RS_STRAIGHT:
-                    for m in range(3):
-                        value = value + parts[l, at, m].astype(F32)
-                else:
-                    value = value + parts[l, at, 0].astype(F32) + parts[l, 1 - at, 2].astype(F32)
+                for m in range(3):
+                    value = value + parts[l, at, m].astype(F32)
                 total[l, half] = value.astype(BF16)
             for m in range(1, n_blk):
-                links.push(total.at[l, z ^ m], r["RZ_" + kind].at[l, m - 1], rs_out[kind][1], rs_recv[kind, l][2], (z ^ m, w))
+                links.push(total.at[l, z ^ m], r["RZ_" + kind].at[l, m - 1], rs_out[kind][1], rs_recv[kind, l][1], (z ^ m, w))
 
         def rs_end(kind, l):
             total = r["SZ_" + kind][l, z].astype(F32)
-            links.arrived(r["RZ_" + kind].at[l], rs_recv[kind, l][2])
+            links.arrived(r["RZ_" + kind].at[l], rs_recv[kind, l][1])
             for m in range(1, n_blk):
                 total = total + r["RZ_" + kind][l, m - 1].astype(F32)
             return total
@@ -873,9 +849,6 @@
             rs_start("d", l)
             store_grad("i", l, tn(Y1B[l], DF[...]))
             rs_start("i", l)
-            if l < LAYERS - 1:
-                rs_pass("q", l + 1)
-                rs_z("d", l + 1)
             gain = wide(l, ROW_G1)
             sums = [jnp.zeros((8, D), F32) for _ in range(3)]
             for chunk in range(CHUNKS):
@@ -910,9 +883,6 @@
                 r["G_o"][l, c] = own_part
                 r["G_o"][l, 1 - c] = other_part
             rs_start("o", l)
-            if l < LAYERS - 1:
-                rs_z("i", l + 1)
-                small_z(l + 1)
             keys, values = QKV[l, :, 128:256], QKV[l, :, 256:384]
             for chunk in range(CHUNKS):
                 rows = rows_of(chunk)
@@ -929,17 +899,9 @@
                     d_query.append(nn(KT[l, head], DS[h, :, rows]))
                 d_query = jnp.concatenate(d_query, axis=0) * 0.125
                 DQKV[rows, 0:128] = d_query.T.astype(BF16)
-                if l == LAYERS - 1:
-                    if chunk == CHUNKS - 1:
-                        rs_pass("d", l)
-                elif chunk == -1:
-                    rs_z("o", l + 1)
-                    rs_pass("d", l)
-                elif chunk == CHUNKS - 1:
-                    rs_z("o", l + 1)
-                    rs_pass("d", l)
-                    rs_z("q", l + 1)
-                    rs_pass("i", l)
+                if l < LAYERS - 1:
+                    rs_z("d", 1)
+                    rs_z("i", 1)
             d_keys = jnp.zeros((SEQ, 128), F32)
             d_values = jnp.zeros((SEQ, 128), F32)
             for h in (0, 1):
@@ -964,21 +926,21 @@
             SGL[l, SG_BQ : SG_BQ + 1, :] = column_sum(fold(DQKV[:, 0:128].astype(F32)))
             SGL[l, SG_BV : SG_BV + 1, :] = column_sum(fold(DQKV[:, 256:384].astype(F32)))
             small_start(l)
-            if l == LAYERS - 1:
-                rs_pass("i", l)
-            rs_pass("o", l)
+            if l < LAYERS - 1:
+                rs_z("o", 1)
+                rs_z("q", 1)
+                small_z(1)
         for chunk in range(CHUNKS):
             take(step + 1, chunk)
             for t in range(0, HALF, BS):
                 tile = slice(chunk * HALF + t, chunk * HALF + t + BS)
                 grad = DY[tile] + PRECV[step + 1, tile].astype(F32)
                 YB[1][(chunk * HALF + t) // BS] = grad.astype(BF16)
-        rs_z("d", 0)
-        rs_z("i", 0)
         send_back(1)
         SGF = r["SGF"]
         if gather:
-            rs_pass("q", 0)
+            rs_z("d", 0)
+            rs_z("i", 0)
             rs_z("o", 0)
             small_z(0)
             FX, RX = r["FX"], r["RX"]

time: 71 us -> 69.3 us (0.976)
  Pallas kernels: 69.4 us -> 67.7 us
    pallas_call x1, Pallas kernels: 68.4 us -> 66.8 us  [call_kernel(): pl.pallas_call(kernel, out_shape=[hold(shape, F32) for shape in shapes.va...]
where the time goes in v3:
time: 69.3 us; the launch traced here: 69.2 us
  Pallas kernels  67.7 us (98%)
  between operations  1.46 us (2%)
    pallas_call x1, Pallas kernels, call_kernel(): pl.pallas_call(kernel, out_shape=[hold(shape, F32) for shape in shapes.va...  66.8 us

profile of v3, /device:TPU:1, one launch (start us, length us, event | category | flops | bytes accessed | tf_op | source)
XLA Modules:
  0.0 69.2 jit_solution(5839252422907305070)
XLA Ops:
  1.3 66.8 %encoder.1 = (f32[4,64,256]{2,1,0:T(8,128)S(1)}, f32[4,64,256]{2,1,0:T(8,128)S(1)}, f32[2,8,768]{2,1,0:T(8,128)S(1)}, f32[2,8,256]{2,1,0:T(8,128)S(1)}, f32[2,8,...) custom-call(bf16[4,64,256]{2,1,0:T(8,128)(2,1)} %bitcast.5, ...), custom_call_target="tpu_custom_call" | custom-call | tf_op jit(solution)/shard_map/encoder/pallas_call | solution.py:1082
  68.1 0.9 %write_out.1 = (f32[4,64,256]{2,1,0:T(8,128)}, f32[4,64,256]{2,1,0:T(8,128)}, f32[2,8,768]{2,1,0:T(8,128)}, f32[2,8,256]{2,1,0:T(8,128)}, f32[2,8,1024]{2,1,0:T(...) custom-call(f32[4,64,256]{2,1,0:T(8,128)S(1)} %get-tuple-element.27.refs_0_, ...), custom_call_target="tpu_custom_call" | custom-call | tf_op jit(solution)/shard_map/write_out/pallas_call | solution.py:1094

commit v4 on v3

--- a/solution.py
+++ b/solution.py
@@ -203,6 +203,7 @@
         R2=vmem((LAYERS, SEQ, 1), F32),
         Y1B=vmem((LAYERS, SEQ, D), BF16),
         FS=vmem((HALF, MY_FF), F32),
+        CDF=vmem((HALF, MY_FF), F32),
         G=vmem((LAYERS, SEQ, MY_FF), BF16),
         GP=vmem((LAYERS, SEQ, MY_FF), BF16),
         DY=vmem((SEQ, D), F32),
@@ -688,11 +689,16 @@
                     inner = FS[t : t + 32] + inner_bias
                     below = 0.5 + 0.5 * lax.erf(inner * 0.7071067811865476)
                     G[l, tile] = (inner * below).astype(BF16)
-                    slope = below + inner * (jnp.exp(inner * inner * -0.5) * 0.3989422804014327)
-                    GP[l, tile] = slope.astype(BF16)
+                    FS[t : t + 32] = inner
+                    r["CDF"][t : t + 32] = below
                 branch = nn(G[l, rows], weight(2, l))
                 give(step + 1, chunk, branch)
                 PO[rows] = X[rows] + branch + wide(l, ROW_BD)
+                for t in range(0, FWD, 32):
+                    tile = slice(chunk * FWD + t, chunk * FWD + t + 32)
+                    inner = FS[t : t + 32]
+                    bell = jnp.exp(inner * inner * -0.5) * 0.3989422804014327
+                    GP[l, tile] = (r["CDF"][t : t + 32] + inner * bell).astype(BF16)
             if gather and l + 1 < LAYERS:
                 ag_pass((1, l + 1))
                 ag_pass((2, l + 1))

time: 69.3 us -> 69.1 us (level)
  no operation moved by 1% of the time
where the time goes in v4:
time: 69.1 us; the launch traced here: 69 us
  Pallas kernels  67.5 us (98%)
  between operations  1.46 us (2%)
    pallas_call x1, Pallas kernels, call_kernel(): pl.pallas_call(kernel, out_shape=[hold(shape, F32) for shape in shapes.va...  66.6 us

profile of v4, /device:TPU:1, one launch (start us, length us, event | category | flops | bytes accessed | tf_op | source)
XLA Modules:
  0.0 69.0 jit_solution(11692392592006790935)
XLA Ops:
  1.3 66.6 %encoder.1 = (f32[4,64,256]{2,1,0:T(8,128)S(1)}, f32[4,64,256]{2,1,0:T(8,128)S(1)}, f32[2,8,768]{2,1,0:T(8,128)S(1)}, f32[2,8,256]{2,1,0:T(8,128)S(1)}, f32[2,8,...) custom-call(bf16[4,64,256]{2,1,0:T(8,128)(2,1)} %bitcast.5, ...), custom_call_target="tpu_custom_call" | custom-call | tf_op jit(solution)/shard_map/encoder/pallas_call | solution.py:1088
  67.9 0.9 %write_out.1 = (f32[4,64,256]{2,1,0:T(8,128)}, f32[4,64,256]{2,1,0:T(8,128)}, f32[2,8,768]{2,1,0:T(8,128)}, f32[2,8,256]{2,1,0:T(8,128)}, f32[2,8,1024]{2,1,0:T(...) custom-call(f32[4,64,256]{2,1,0:T(8,128)S(1)} %get-tuple-element.27.refs_0_, ...), custom_call_target="tpu_custom_call" | custom-call | tf_op jit(solution)/shard_map/write_out/pallas_call | solution.py:1100
